TPU v7x, 256 devices: a whole 4x4x8 slice. The times are simulated.
256 devices in a mesh: dp: 32 (over x, y, core), ctx: 8 (over z).
Axes of the slice: x: 4, y: 4, z: 8, core: 2. Of those that a mesh axis runs over, the one named last changes fastest.
Arguments:
- queries: bfloat16 [32768, 32, 128], P(('ctx', 'dp')), may hold values from -8 to 8
- keys: bfloat16 [32768, 8, 128], P(('ctx', 'dp')), may hold values from -8 to 8
- values: bfloat16 [32768, 8, 128], P(('ctx', 'dp')), may hold values from -6 to 6
- doc_blocks: int32 [32], replicated, may hold values from 1 to 16, 256 in all
Outputs:
- attended: bfloat16 [32768, 32, 128], P(('ctx', 'dp'))
Inputs may be any that keep to these rules, and one draw needn't show every extreme that they name: `doc_blocks`: lengths in blocks of 128 tokens; they sum to 256 and the longest is exactly 16.
All inputs are finite; a program needn't handle non-finite values.
Results may differ from a plain program's by a relative error of at most 0.0037.
Values may be sent and summed in bfloat16 or wider, within the bound.
A program may use at most 128 MiB of HBM per device.

v0:
```python
import jax
import jax.numpy as jnp
from jax import lax
from jax.sharding import PartitionSpec as P

BLK = 128


def passed_along(block, axis, distance):
    devices = range(lax.axis_size(axis))
    route = [(i - distance, i) for i in devices if i - distance in devices]
    return lax.ppermute(block, axis, route)


def token_docs(doc_blocks, first_block, count, block):
    doc_ends = jnp.cumsum(doc_blocks, dtype=jnp.int32)
    blocks = first_block + jnp.arange(count, dtype=jnp.int32)
    owners = jnp.sum(
        (doc_ends[None, :] <= blocks[:, None]).astype(jnp.int32), axis=1, dtype=jnp.int32
    )
    owners = jnp.where(blocks < 0, -1, owners)
    return jnp.repeat(owners, block)


def attend(query_tiles, offsets, key_buffer, value_buffer, key_docs, key_span):
    tile_rows = query_tiles.shape[1]
    width = key_span + tile_rows
    score_scale = query_tiles.shape[-1] ** (-0.5)
    causal = jnp.arange(width)[None, :] <= key_span + jnp.arange(tile_rows)[:, None]

    def one_tile(packed):
        query_tile, offset = packed
        key_window = lax.dynamic_slice_in_dim(key_buffer, offset, width, 0)
        value_window = lax.dynamic_slice_in_dim(value_buffer, offset, width, 0)
        window_docs = lax.dynamic_slice_in_dim(key_docs, offset, width, 0)
        query_docs = lax.dynamic_slice_in_dim(key_docs, offset + key_span, tile_rows, 0)
        allowed = (window_docs[None, :] == query_docs[:, None]) & causal
        scores = (
            jnp.einsum("qhd,kd->hqk", query_tile, key_window, preferred_element_type=jnp.float32)
            * score_scale
        )
        scores = jnp.where(allowed[None], scores, -jnp.inf)
        row_max = jnp.max(scores, axis=2, keepdims=True)
        weights = jnp.exp(scores - row_max)
        totals = jnp.sum(weights, axis=2)
        combined = jnp.einsum(
            "hqk,kd->qhd",
            weights.astype(jnp.bfloat16),
            value_window,
            preferred_element_type=jnp.float32,
        )
        return (combined / jnp.transpose(totals)[:, :, None]).astype(jnp.bfloat16)

    return lax.map(one_tile, (query_tiles, offsets))


def on_device(queries, keys, values, doc_blocks):
    tok_rows, head_count, head_size = queries.shape
    kv_heads = keys.shape[1]
    dp_count = lax.axis_size("dp")
    ctx_count = lax.axis_size("ctx")
    ctx_index = lax.axis_index("ctx")
    region = tok_rows * dp_count
    tile_rows = region // ctx_count
    key_span = region // 2
    heads_here = head_count // dp_count
    sharing = dp_count // kv_heads
    key_copies = jnp.repeat(keys, sharing, axis=1)
    value_copies = jnp.repeat(values, sharing, axis=1)
    query_local, key_local, value_local = (
        lax.all_to_all(queries, "dp", split_axis=1, concat_axis=0, tiled=True),
        lax.all_to_all(key_copies, "dp", split_axis=1, concat_axis=0, tiled=True),
        lax.all_to_all(value_copies, "dp", split_axis=1, concat_axis=0, tiled=True),
    )
    key_local = key_local.reshape(region, head_size)
    value_local = value_local.reshape(region, head_size)
    query_tiles = query_local.reshape(ctx_count, tile_rows, heads_here, head_size)
    key_tail = key_local[region - key_span :]
    value_tail = value_local[region - key_span :]
    key_before, value_before = passed_along((key_tail, value_tail), "ctx", 1)
    key_buffer = jnp.concatenate([key_before, key_local], axis=0)
    value_buffer = jnp.concatenate([value_before, value_local], axis=0)
    key_docs = token_docs(
        doc_blocks, (ctx_index * region - key_span) // BLK, (key_span + region) // BLK, BLK
    )
    offsets = jnp.arange(ctx_count, dtype=jnp.int32) * tile_rows
    output_tiles = attend(query_tiles, offsets, key_buffer, value_buffer, key_docs, key_span)
    output_region = output_tiles.reshape(region, heads_here, head_size)
    return lax.all_to_all(output_region, "dp", split_axis=0, concat_axis=1, tiled=True)


def solution(mesh):
    placed = (
        P(("ctx", "dp"), None, None),
        P(("ctx", "dp"), None, None),
        P(("ctx", "dp"), None, None),
        P(),
    )
    return jax.shard_map(
        on_device,
        mesh=mesh,
        in_specs=placed,
        out_specs=P(("ctx", "dp"), None, None),
        check_vma=False,
    )
```

profile of v0, /device:TPU:99, one launch (start us, length us, event | category | flops | bytes accessed | tf_op | source)
XLA Modules:
  0.0 177.0 jit_solution(14272578801299333512)
XLA Ops:
  0.0 1.0 copy.26
  1.0 1.2 broadcast_in_dim.42
  2.2 8.1 %all-to-all-start.1 = ((bf16[128,32,128]{2,0,1:T(8,128)(2,1)}), bf16[128,32,128]{2,0,1:T(8,128)(2,1)S(1)}, u32[]{:S(2)}, u32[]{:S(2)}) async-start(bf16[128,32,128]{2,0,1:T(8,128)(2,1)} %bitcast.8), calls=%async_computation.1 | async-start | bytes 2097152 | tf_op jit(solution)/shard_map/all_to_all | solution.py:72
  10.4 15.1 %all-to-all-done.1 = bf16[128,32,128]{2,0,1:T(8,128)(2,1)S(1)} async-done(((bf16[128,32,128]{2,0,1:T(8,128)(2,1)}), bf16[128,32,128]{2,0,1:T(8,128)(2,1)S(1)}, u32[]{:S(2)}, u32[]{:S(2)}) %all-to-all-start.1) | async-done | bytes 1048608 | tf_op jit(solution)/shard_map/all_to_all | solution.py:72
  25.5 1.2 broadcast_in_dim.39
  26.7 5.7 %all-to-all-start = ((bf16[128,32,128]{2,0,1:T(8,128)(2,1)}), bf16[128,32,128]{2,0,1:T(8,128)(2,1)S(1)}, u32[]{:S(2)}, u32[]{:S(2)}) async-start(bf16[128,32,128]{2,0,1:T(8,128)(2,1)} %bitcast.84), calls=%async_computation | async-start | bytes 2097152 | tf_op jit(solution)/shard_map/all_to_all | solution.py:73
  32.7 2.6 %copy.27 = bf16[128,32,128]{2,0,1:T(8,128)(2,1)} copy(bf16[128,32,128]{2,1,0:T(8,128)(2,1)} %param.6) | data formatting | bytes 2097152 | tf_op args[0]
  35.5 4.8 %collective-permute-start.1 = (bf16[2048,128]{1,0:T(8,128)(2,1)S(1)}, bf16[2048,128]{1,0:T(8,128)(2,1)S(1)}, u32[]{:S(2)}, u32[]{:S(2)}) collective-permute-start(bf16[2048,128]{1,0:T(8,128)(2,1)S(1)} %bitcast.85), channel_id=1, source_target_pairs={{0,1},{1,2},{2,3},{3,4},{4,5},{5,6},{6,7},{8,9},{9,10},{10,11},{11... | collective-permute-start | bytes 1572872 | tf_op jit(solution)/shard_map/ppermute | solution.py:12
  40.4 7.2 %all-to-all-done = bf16[128,32,128]{2,0,1:T(8,128)(2,1)S(1)} async-done(((bf16[128,32,128]{2,0,1:T(8,128)(2,1)}), bf16[128,32,128]{2,0,1:T(8,128)(2,1)S(1)}, u32[]{:S(2)}, u32[]{:S(2)}) %all-to-all-start) | async-done | bytes 1048608 | tf_op jit(solution)/shard_map/all_to_all | solution.py:73
  47.6 6.2 %all-to-all-start.2 = ((bf16[128,32,128]{2,0,1:T(8,128)(2,1)}), bf16[128,32,128]{2,0,1:T(8,128)(2,1)}, u32[]{:S(2)}, u32[]{:S(2)}) async-start(bf16[128,32,128]{2,0,1:T(8,128)(2,1)} %copy.27), calls=%async_computation.2 | async-start | bytes 2097152 | tf_op jit(solution)/shard_map/all_to_all | solution.py:71
  53.8 4.8 %collective-permute-start = (bf16[2048,128]{1,0:T(8,128)(2,1)S(1)}, bf16[2048,128]{1,0:T(8,128)(2,1)S(1)}, u32[]{:S(2)}, u32[]{:S(2)}) collective-permute-start(bf16[2048,128]{1,0:T(8,128)(2,1)S(1)} %bitcast.86), channel_id=1, source_target_pairs={{0,1},{1,2},{2,3},{3,4},{4,5},{5,6},{6,7},{8,9},{9,10},{10,11},{11... | collective-permute-start | bytes 1572872 | tf_op jit(solution)/shard_map/ppermute | solution.py:12
  58.6 1.3 pad_maximum_fusion.1
  59.8 9.7 %collective-permute-done = bf16[2048,128]{1,0:T(8,128)(2,1)S(1)} collective-permute-done((bf16[2048,128]{1,0:T(8,128)(2,1)S(1)}, bf16[2048,128]{1,0:T(8,128)(2,1)S(1)}, u32[]{:S(2)}, u32[]{:S(2)}) %collective-permute-start) | collective-permute-done | bytes 524320 | tf_op jit(solution)/shard_map/ppermute | solution.py:12
  69.6 77.7 %while.13 = (s32[]{:T(128)}, bf16[8,512,1,128]{3,1,0,2:T(8,128)(2,1)}, s32[8]{0:T(128)S(1)}, bf16[6144,128]{1,0:T(8,128)(2,1)S(1)}, s32[6144]{0:T(1024)S(1)}, /*...) while((s32[]{:T(128)}, ...), condition=%wide.region_5.6_spmd.clone, body=%wide.region_2.5_spmd.clone.sunk | while | flops 684325888 | bytes 17876200 | solution.py:54
  73.5 3.2 %fusion.36 = (f32[512]{0:T(512)S(1)}, f32[1,512,2560]{1,2,0:T(8,128)S(1)}) fusion(bf16[8,512,1,128]{3,1,2,0:T(8,128)(2,1)} %get-tuple-element.253, s32[]{:T(128)} %get-tuple-element.234, bf16[6144,128]{1,0:T(8,128)(2,1)} %get-tuple-element.252, s32[]{:T(128)S(6)} %select_n.39, s32[512]{0:T(512)S(1)} %get-tuple-element.254, ...), kind=kOutput, calls=%fused_computation.30.clone.1 | convolution fusion | flops 343408128 | bytes 6046212 | tf_op jit(solution)/shard_map/while/body/eval_jaxpr/qhd,kd->hqk/dot_general | solution.py:39
  76.7 0.8 fusion.37
  77.5 1.1 fusion.38
  78.7 0.7 constant_dynamic-update-slice_fusion.2
  83.2 3.2 %fusion.36 = (f32[512]{0:T(512)S(1)}, f32[1,512,2560]{1,2,0:T(8,128)S(1)}) fusion(bf16[8,512,1,128]{3,1,2,0:T(8,128)(2,1)} %get-tuple-element.253, s32[]{:T(128)} %get-tuple-element.234, bf16[6144,128]{1,0:T(8,128)(2,1)} %get-tuple-element.252, s32[]{:T(128)S(6)} %select_n.39, s32[512]{0:T(512)S(1)} %get-tuple-element.254, ...), kind=kOutput, calls=%fused_computation.30.clone.1 | convolution fusion | flops 343408128 | bytes 6046212 | tf_op jit(solution)/shard_map/while/body/eval_jaxpr/qhd,kd->hqk/dot_general | solution.py:39
  86.4 0.8 fusion.37
  87.2 1.1 fusion.38
  88.4 0.7 constant_dynamic-update-slice_fusion.2
  92.9 3.2 %fusion.36 = (f32[512]{0:T(512)S(1)}, f32[1,512,2560]{1,2,0:T(8,128)S(1)}) fusion(bf16[8,512,1,128]{3,1,2,0:T(8,128)(2,1)} %get-tuple-element.253, s32[]{:T(128)} %get-tuple-element.234, bf16[6144,128]{1,0:T(8,128)(2,1)} %get-tuple-element.252, s32[]{:T(128)S(6)} %select_n.39, s32[512]{0:T(512)S(1)} %get-tuple-element.254, ...), kind=kOutput, calls=%fused_computation.30.clone.1 | convolution fusion | flops 343408128 | bytes 6046212 | tf_op jit(solution)/shard_map/while/body/eval_jaxpr/qhd,kd->hqk/dot_general | solution.py:39
  96.1 0.8 fusion.37
  96.9 1.1 fusion.38
  98.1 0.7 constant_dynamic-update-slice_fusion.2
  102.6 3.2 %fusion.36 = (f32[512]{0:T(512)S(1)}, f32[1,512,2560]{1,2,0:T(8,128)S(1)}) fusion(bf16[8,512,1,128]{3,1,2,0:T(8,128)(2,1)} %get-tuple-element.253, s32[]{:T(128)} %get-tuple-element.234, bf16[6144,128]{1,0:T(8,128)(2,1)} %get-tuple-element.252, s32[]{:T(128)S(6)} %select_n.39, s32[512]{0:T(512)S(1)} %get-tuple-element.254, ...), kind=kOutput, calls=%fused_computation.30.clone.1 | convolution fusion | flops 343408128 | bytes 6046212 | tf_op jit(solution)/shard_map/while/body/eval_jaxpr/qhd,kd->hqk/dot_general | solution.py:39
  105.8 0.8 fusion.37
  106.6 1.1 fusion.38
  112.3 3.2 %fusion.36 = (f32[512]{0:T(512)S(1)}, f32[1,512,2560]{1,2,0:T(8,128)S(1)}) fusion(bf16[8,512,1,128]{3,1,2,0:T(8,128)(2,1)} %get-tuple-element.253, s32[]{:T(128)} %get-tuple-element.234, bf16[6144,128]{1,0:T(8,128)(2,1)} %get-tuple-element.252, s32[]{:T(128)S(6)} %select_n.39, s32[512]{0:T(512)S(1)} %get-tuple-element.254, ...), kind=kOutput, calls=%fused_computation.30.clone.1 | convolution fusion | flops 343408128 | bytes 6046212 | tf_op jit(solution)/shard_map/while/body/eval_jaxpr/qhd,kd->hqk/dot_general | solution.py:39
  115.5 0.8 fusion.37
  116.3 1.1 fusion.38
  117.5 0.7 constant_dynamic-update-slice_fusion.2
  122.0 3.2 %fusion.36 = (f32[512]{0:T(512)S(1)}, f32[1,512,2560]{1,2,0:T(8,128)S(1)}) fusion(bf16[8,512,1,128]{3,1,2,0:T(8,128)(2,1)} %get-tuple-element.253, s32[]{:T(128)} %get-tuple-element.234, bf16[6144,128]{1,0:T(8,128)(2,1)} %get-tuple-element.252, s32[]{:T(128)S(6)} %select_n.39, s32[512]{0:T(512)S(1)} %get-tuple-element.254, ...), kind=kOutput, calls=%fused_computation.30.clone.1 | convolution fusion | flops 343408128 | bytes 6046212 | tf_op jit(solution)/shard_map/while/body/eval_jaxpr/qhd,kd->hqk/dot_general | solution.py:39
  125.2 0.8 fusion.37
  126.0 1.1 fusion.38
  127.2 0.7 constant_dynamic-update-slice_fusion.2
  131.8 3.2 %fusion.36 = (f32[512]{0:T(512)S(1)}, f32[1,512,2560]{1,2,0:T(8,128)S(1)}) fusion(bf16[8,512,1,128]{3,1,2,0:T(8,128)(2,1)} %get-tuple-element.253, s32[]{:T(128)} %get-tuple-element.234, bf16[6144,128]{1,0:T(8,128)(2,1)} %get-tuple-element.252, s32[]{:T(128)S(6)} %select_n.39, s32[512]{0:T(512)S(1)} %get-tuple-element.254, ...), kind=kOutput, calls=%fused_computation.30.clone.1 | convolution fusion | flops 343408128 | bytes 6046212 | tf_op jit(solution)/shard_map/while/body/eval_jaxpr/qhd,kd->hqk/dot_general | solution.py:39
  134.9 0.8 fusion.37
  135.7 1.1 fusion.38
  141.5 3.2 %fusion.36 = (f32[512]{0:T(512)S(1)}, f32[1,512,2560]{1,2,0:T(8,128)S(1)}) fusion(bf16[8,512,1,128]{3,1,2,0:T(8,128)(2,1)} %get-tuple-element.253, s32[]{:T(128)} %get-tuple-element.234, bf16[6144,128]{1,0:T(8,128)(2,1)} %get-tuple-element.252, s32[]{:T(128)S(6)} %select_n.39, s32[512]{0:T(512)S(1)} %get-tuple-element.254, ...), kind=kOutput, calls=%fused_computation.30.clone.1 | convolution fusion | flops 343408128 | bytes 6046212 | tf_op jit(solution)/shard_map/while/body/eval_jaxpr/qhd,kd->hqk/dot_general | solution.py:39
  144.7 0.8 fusion.37
  145.4 1.1 fusion.38
  146.7 0.7 constant_dynamic-update-slice_fusion.2
  147.9 2.7 %reduce.9 = bf16[4096,128]{1,0:T(8,128)(2,1)S(1)} reduce(bf16[4096,1,128]{2,0,1:T(8,128)(2,1)} %bitcast.18, bf16[]{:T(256)} %broadcast.77), dimensions={1}, to_apply=%copy.30.reduce_sub_computation | reduce | bytes 2097154 | tf_op jit(solution)/shard_map/reshape | solution.py:88
  150.9 23.3 %all_to_all.63 = bf16[32,2,8192]{2,1,0:T(2,128)(2,1)S(1)} all-to-all(bf16[32,2,8192]{2,1,0:T(2,128)(2,1)S(1)} %reshape.160), channel_id=1, replica_groups=mesh['dp'=32,'ctx'=8] {'dp'}, dimensions={0} | all-to-all | bytes 2097152 | tf_op jit(solution)/shard_map/all_to_all | solution.py:89
  174.2 1.0 reshape.161
  175.4 1.6 copy.31
  (57 shorter events, 9.9 us)
Async XLA Ops:
  0.0 10.3 %copy-start = (bf16[128,8,128]{2,1,0:T(8,128)(2,1)S(1)}, bf16[128,8,128]{2,1,0:T(8,128)(2,1)}, u32[]{:S(2)}) copy-start(bf16[128,8,128]{2,1,0:T(8,128)(2,1)} %param.8) | copy-start | bytes 786436
  2.2 30.2 %copy-start.1 = (s32[32]{0:T(128)S(1)}, s32[32]{0:T(128)}, u32[]{:S(2)}) copy-start(s32[32]{0:T(128)} %param.9) | copy-start | bytes 388
  2.2 23.3 %all-to-all-start.1 = ((bf16[128,32,128]{2,0,1:T(8,128)(2,1)}), bf16[128,32,128]{2,0,1:T(8,128)(2,1)S(1)}, u32[]{:S(2)}, u32[]{:S(2)}) async-start(bf16[128,32,128]{2,0,1:T(8,128)(2,1)} %bitcast.8), calls=%async_computation.1 | async-start | bytes 2097152 | tf_op jit(solution)/shard_map/all_to_all | solution.py:72
  26.7 20.9 %all-to-all-start = ((bf16[128,32,128]{2,0,1:T(8,128)(2,1)}), bf16[128,32,128]{2,0,1:T(8,128)(2,1)S(1)}, u32[]{:S(2)}, u32[]{:S(2)}) async-start(bf16[128,32,128]{2,0,1:T(8,128)(2,1)} %bitcast.84), calls=%async_computation | async-start | bytes 2097152 | tf_op jit(solution)/shard_map/all_to_all | solution.py:73
  35.5 23.1 %collective-permute-start.1 = (bf16[2048,128]{1,0:T(8,128)(2,1)S(1)}, bf16[2048,128]{1,0:T(8,128)(2,1)S(1)}, u32[]{:S(2)}, u32[]{:S(2)}) collective-permute-start(bf16[2048,128]{1,0:T(8,128)(2,1)S(1)} %bitcast.85), channel_id=1, source_target_pairs={{0,1},{1,2},{2,3},{3,4},{4,5},{5,6},{6,7},{8,9},{9,10},{10,11},{11... | collective-permute-start | bytes 1572872 | tf_op jit(solution)/shard_map/ppermute | solution.py:12
  47.6 22.0 %all-to-all-start.2 = ((bf16[128,32,128]{2,0,1:T(8,128)(2,1)}), bf16[128,32,128]{2,0,1:T(8,128)(2,1)}, u32[]{:S(2)}, u32[]{:S(2)}) async-start(bf16[128,32,128]{2,0,1:T(8,128)(2,1)} %copy.27), calls=%async_computation.2 | async-start | bytes 2097152 | tf_op jit(solution)/shard_map/all_to_all | solution.py:71
  53.8 15.7 %collective-permute-start = (bf16[2048,128]{1,0:T(8,128)(2,1)S(1)}, bf16[2048,128]{1,0:T(8,128)(2,1)S(1)}, u32[]{:S(2)}, u32[]{:S(2)}) collective-permute-start(bf16[2048,128]{1,0:T(8,128)(2,1)S(1)} %bitcast.86), channel_id=1, source_target_pairs={{0,1},{1,2},{2,3},{3,4},{4,5},{5,6},{6,7},{8,9},{9,10},{10,11},{11... | collective-permute-start | bytes 1572872 | tf_op jit(solution)/shard_map/ppermute | solution.py:12
where the time goes:
time: 180 us; the launch traced here: 177 us
  matrix products  34.3 us (19%)
  waiting for transfers between devices  32 us (18%)
  starting transfers between devices  29.4 us (16%)
  loops' own time  25 us (14%)
  blocking collectives  23.3 us (13%)
  local copies, waits for them, and re-layouts  22.4 us (12%)
  other arithmetic  10.5 us (6%)
    dot_general x8, matrix products, one_tile(): jnp.einsum('qhd,kd->hqk', query_tile, key_window, preferred_element_type=...  25.5 us
    another operation x1, loops' own time, attend(): return lax.map(one_tile, (query_tiles, offsets))  25 us
    all_to_all x1, blocking collectives, on_device(): lax.all_to_all(output_region, 'dp', split_axis=0, concat_axis=1, tiled=True)  23.3 us
    all_to_all x1, waiting for transfers between devices, on_device(): lax.all_to_all(key_copies, 'dp', split_axis=1, concat_axis=0, tiled=True)  15.1 us
    ppermute x2, waiting for transfers between devices, passed_along(): return lax.ppermute(block, axis, route)  9.66 us
    ppermute x2, starting transfers between devices, passed_along(): return lax.ppermute(block, axis, route)  9.51 us
    dot_general x8, matrix products, one_tile(): jnp.einsum('hqk,kd->qhd', weights.astype(jnp.bfloat16), value_window, pre...  8.79 us
    all_to_all x1, starting transfers between devices, on_device(): lax.all_to_all(key_copies, 'dp', split_axis=1, concat_axis=0, tiled=True)  8.07 us
  transfers between devices with their start and end apart: 5, of which 3 were waited for; matrix products, arithmetic and copies ran while one was open for 3% of the time, Pallas kernels for 0%

commit v1 on v0

v1 whole, which is shorter than its diff:
```python
import jax
import jax.numpy as jnp
from jax import lax
from jax.experimental import pallas as pl
from jax.experimental.pallas import tpu as pltpu
from jax.sharding import PartitionSpec as P

PIECES = 4
SEND_ORDER = (3, 0, 1, 2)
STEPS = (
    (215088, 5445680, 5445680, 202800),
    (2115584, 8389172, 8389428, 3359795),
    (6500401, 2114817, 2114817, 4200448),
    (2181136, 8454707, 8454707, 3162115),
    (2109697, 2180369, 2180369, 4266000),
    (149536, 8519683, 8519683, 3227667),
    (204817, 3294241, 2244897, 4331552),
    (229431, 8242, 4399635, 3294755),
    (6369569, 229429, 2326581, 28722),
    (6434824, 21523, 4202530, 3375159),
    (94517, 2241032, 2129925, 217349),
    (4202520, 1134626, 73763, 3178550),
    (159751, 73752, 98325, 1134594),
    (139304, 1200182, 151607, 3244055),
    (24837, 2322472, 2261046, 24594),
    (222226, 28695, 24583, 3309607),
    (90389, 2256902, 94230, 151586),
    (155685, 155670, 2256934, 155670),
)
OWN_SENDS = (
    (15, 13, 13, 12),
    (15, 13, 13, 12),
    (15, 13, 13, 12),
    (15, 13, 13, 12),
)
SENT = (
    (9, 10, 9, 8),
    (10, 9, 9, 8),
    (9, 10, 9, 8),
    (10, 9, 9, 8),
)
DIRS = 4
BLK = 128
HD = 128
LOG2E = 1.4426950408889634
MASKED = -1e30
MESH = pl.DeviceIdType.MESH


def of_y(y, row):
    value = jnp.int32(row[3])
    for i in range(3):
        value = jnp.where(y == i, jnp.int32(row[i]), value)
    return value


def kernel(
    q_ref, k_ref, v_ref, docs_ref, o_ref,
    own, sib, transit, qf, kf, vf, qs, acc, top,
    send_sem, pair_sem, own_sem, sib_sem, transit_sem,
):
    tokens, q_heads, _ = q_ref.shape
    kv_heads = k_ref.shape[1]
    group = q_heads // kv_heads
    rows = group * tokens
    per_part = kv_heads // PIECES
    parts = PIECES
    dp = lax.axis_index("dp")
    z = lax.axis_index("ctx")
    x, y, core = dp // 8, (dp // 2) % 4, dp % 2

    def at(to_x, to_y, to_z, to_core):
        return ((to_x % 4) * 8 + (to_y % 4) * 2 + to_core, to_z % 8)

    def one_if(condition):
        return jnp.where(condition, jnp.int32(1), jnp.int32(0))

    up = at(x, y + 1, z, core)
    down = at(x, y + 3, z, core)
    ahead = at(x + 1, y, z + one_if(x == 3), core)
    behind = at(x + 3, y, z + 8 - one_if(x == 0), core)
    through = at(x + 3, y, z, core)
    through_from = at(x + 1, y, z, core)
    beyond = at(x + 3, y, z + one_if((x == 1) | (x == 2)), core)
    beyond_from = at(x + 1, y, z + 8 - one_if(x <= 1), core)
    pair = at(x, y, z, 1 - core)
    targets = (up, down, ahead)
    shifts = (jnp.where(y == 3, jnp.int32(-3), jnp.int32(1)), jnp.where(y == 0, jnp.int32(3), jnp.int32(-1)), jnp.int32(4))

    kf[...] = k_ref[...].astype(jnp.float32).reshape(tokens * kv_heads, HD)
    vf[...] = v_ref[...].astype(jnp.float32).reshape(tokens * kv_heads, HD)
    for p in range(parts):
        for i in range(per_part):
            head = pl.ds(p * per_part + i, tokens, stride=kv_heads)
            own[p, pl.ds(i * BLK, BLK), :] = kf[head, :].astype(jnp.bfloat16)
            own[p, pl.ds((per_part + i) * BLK, BLK), :] = vf[head, :].astype(jnp.bfloat16)

    barrier = pltpu.get_barrier_semaphore()
    friends = (up, down, ahead, behind, through, through_from, beyond, beyond_from, pair)
    for friend in friends:
        pl.semaphore_signal(barrier, inc=1, device_id=friend, device_id_type=MESH)
    pl.semaphore_wait(barrier, len(friends))

    def send(src, dst, sem, landed, device):
        pltpu.make_async_remote_copy(
            src_ref=src, dst_ref=dst, send_sem=sem, recv_sem=landed, device_id=device, device_id_type=MESH
        ).start()

    def pass_on(k, p, bits):
        slot = k * parts + p
        for d in range(3):
            @pl.when((bits >> d) % 2 == 1)
            def _():
                to = (k + shifts[d]) * parts + p
                send(own.at[slot], own.at[to], send_sem.at[d], own_sem.at[to], targets[d])
        send(own.at[slot], sib.at[slot], pair_sem, sib_sem.at[slot], pair)

    def await_copy(ref, sem):
        pltpu.make_async_copy(ref, ref, sem).wait()

    for p in SEND_ORDER:
        bits = of_y(y, OWN_SENDS[p])
        send(own.at[p], transit.at[p], send_sem.at[3], transit_sem.at[p], through)
        pass_on(0, p, bits)

    scale = LOG2E * HD**-0.5
    qf[...] = q_ref[...].astype(jnp.float32).reshape(tokens * q_heads, HD)
    for g in range(kv_heads):
        for r in range(group):
            scaled = qf[pl.ds(g * group + r, tokens, stride=q_heads), :] * scale
            high = scaled.astype(jnp.bfloat16)
            qs[g, pl.ds(r * tokens, tokens), pl.ds(0, HD)] = high
            qs[g, pl.ds(r * tokens, tokens), pl.ds(HD, HD)] = (scaled - high.astype(jnp.float32)).astype(jnp.bfloat16)

    block = z * 32 + dp
    end = jnp.int32(0)
    start = jnp.int32(0)
    for i in range(docs_ref.shape[0]):
        end = end + docs_ref[i]
        start = jnp.where(end <= block, end, start)
    reach = block - start

    def bias_of(back):
        return jnp.where((back >= 0) & (back <= reach), jnp.float32(0), jnp.float32(MASKED))

    def sib_back(k):
        return 2 * k + 2 * core - 1

    ones = jnp.ones((2 * BLK, HD), jnp.bfloat16)

    def attend(k, p, bias, first):
        slot = k * parts + p
        for i in range(per_part):
            g = p * per_part + i
            at_keys, at_values = pl.ds(i * BLK, BLK), pl.ds((per_part + i) * BLK, BLK)
            keys = jnp.concatenate([own[slot, at_keys, :], sib[slot, at_keys, :]], axis=0)
            keys = jnp.concatenate([keys, keys], axis=1)
            values = jnp.concatenate([own[slot, at_values, :], sib[slot, at_values, :]], axis=0)
            values = jnp.concatenate([values, ones], axis=1)
            scores = lax.dot_general(
                qs[g], keys, (((1,), (1,)), ((), ())), preferred_element_type=jnp.float32
            )
            scores = scores + bias
            peak = jnp.max(scores, axis=1, keepdims=True)
            if first:
                new_top = jnp.broadcast_to(peak, (rows, BLK))
            else:
                new_top = jnp.maximum(top[g], peak)
            weights = jnp.exp2(scores - jnp.concatenate([new_top, new_top], axis=1))
            summed = jnp.dot(weights.astype(jnp.bfloat16), values, preferred_element_type=jnp.float32)
            if first:
                acc[g] = summed
            else:
                shrink = jnp.exp2(top[g] - new_top)
                acc[g] = acc[g] * jnp.concatenate([shrink, shrink], axis=1) + summed
            top[g] = new_top

    column = lax.broadcasted_iota(jnp.int32, (tokens, 2 * BLK), 1)
    row = lax.broadcasted_iota(jnp.int32, (tokens, 2 * BLK), 0)
    near = jnp.where(
        column < BLK, jnp.where(column <= row, jnp.float32(0), jnp.float32(MASKED)), bias_of(sib_back(0))
    )
    near = jnp.concatenate([near] * group, axis=0)
    for p in SEND_ORDER:
        await_copy(sib.at[p], sib_sem.at[p])
        attend(0, p, near, True)

    lane = lax.broadcasted_iota(jnp.int32, (1, 2 * BLK), 1)

    def attend_far(k, p):
        slot = k * parts + p
        await_copy(sib.at[slot], sib_sem.at[slot])
        bias = jnp.where(lane < BLK, bias_of(2 * k), bias_of(sib_back(k)))
        attend(k, p, bias, False)

    def step(word, half):
        code = (word >> (12 * half)) % 4096
        k, p, bits = code % 16, (code // 16) % 16, code // 256

        @pl.when(k == 0)
        def _():
            await_copy(transit.at[p], transit_sem.at[p])
            to = 8 * parts + p
            send(transit.at[p], own.at[to], send_sem.at[3], own_sem.at[to], beyond)

        @pl.when(k > 0)
        def _():
            slot = k * parts + p
            await_copy(own.at[slot], own_sem.at[slot])
            pass_on(k, p, bits)
        return k, p

    def word_at(index):
        value = jnp.int32(0)
        for i, entry in enumerate(STEPS):
            value = jnp.where(index == i, of_y(y, entry), value)
        return value

    def body(s, before):
        k, p = step(word_at(s // 2), s % 2)

        @pl.when(before[0] > 0)
        def _():
            attend_far(*before)
        return k, p

    last = lax.fori_loop(0, 9 * parts, body, (jnp.int32(0), jnp.int32(0)))

    @pl.when(last[0] > 0)
    def _():
        attend_far(*last)

    for g in range(kv_heads):
        for r in range(group):
            at_rows = pl.ds(r * tokens, tokens)
            result = acc[g, at_rows, pl.ds(0, HD)] / acc[g, at_rows, pl.ds(HD, HD)]
            qf[pl.ds(g * group + r, tokens, stride=q_heads), :] = result
    o_ref[...] = qf[...].reshape(tokens, q_heads, HD).astype(jnp.bfloat16)

    for i in range(4):
        @pl.when(y == i)
        def _():
            for d in range(DIRS):
                sent = own.at[pl.ds(0, SENT[i][d])]
                await_copy(sent, send_sem.at[d])
    await_copy(own, pair_sem)


def on_device(queries, keys, values, doc_blocks):
    tokens, q_heads, _ = queries.shape
    kv_heads = keys.shape[1]
    rows = q_heads // kv_heads * tokens
    part_rows = 2 * (kv_heads // PIECES) * BLK
    vmem = pl.BlockSpec(memory_space=pltpu.VMEM)
    return pl.pallas_call(
        kernel,
        out_shape=jax.ShapeDtypeStruct(queries.shape, jnp.bfloat16),
        in_specs=[vmem, vmem, vmem, pl.BlockSpec(memory_space=pltpu.SMEM)],
        out_specs=vmem,
        scratch_shapes=[
            pltpu.VMEM((9 * PIECES, part_rows, HD), jnp.bfloat16),
            pltpu.VMEM((9 * PIECES, part_rows, HD), jnp.bfloat16),
            pltpu.VMEM((PIECES, part_rows, HD), jnp.bfloat16),
            pltpu.VMEM((tokens * q_heads, HD), jnp.float32),
            pltpu.VMEM((tokens * kv_heads, HD), jnp.float32),
            pltpu.VMEM((tokens * kv_heads, HD), jnp.float32),
            pltpu.VMEM((kv_heads, rows, 2 * HD), jnp.bfloat16),
            pltpu.VMEM((kv_heads, rows, 2 * HD), jnp.float32),
            pltpu.VMEM((kv_heads, rows, BLK), jnp.float32),
            pltpu.SemaphoreType.DMA((DIRS,)),
            pltpu.SemaphoreType.DMA,
            pltpu.SemaphoreType.DMA((9 * PIECES,)),
            pltpu.SemaphoreType.DMA((9 * PIECES,)),
            pltpu.SemaphoreType.DMA((PIECES,)),
        ],
        compiler_params=pltpu.CompilerParams(
            collective_id=0, has_side_effects=True, vmem_limit_bytes=48 << 20
        ),
        name="attend",
    )(queries, keys, values, doc_blocks)


def solution(mesh):
    placed = P(("ctx", "dp"), None, None)
    return jax.shard_map(
        on_device,
        mesh=mesh,
        in_specs=(placed, placed, placed, P()),
        out_specs=placed,
        check_vma=False,
    )
```

time: 180 us -> 74.6 us (0.41); the launches traced: 177 us -> 73.8 us
  Pallas kernels: 0 us -> 69.1 us
  matrix products: 34.3 us -> 0 us
  waiting for transfers between devices: 32 us -> 0 us
  starting transfers between devices: 29.4 us -> 0 us
  loops' own time: 25 us -> 0 us
  blocking collectives: 23.3 us -> 0 us
  local copies, waits for them, and re-layouts: 22.4 us -> 4.75 us
  other arithmetic: 10.5 us -> 0 us
    pallas_call x0 -> x1, Pallas kernels: none -> 69.1 us  [on_device(): pl.pallas_call(kernel, out_shape=jax.ShapeDtypeStruct(queries.shape, jnp....]
    dot_general x16 -> x0, matrix products: 34.3 us -> none  [the longest x8 25.5 us: one_tile(): jnp.einsum('qhd,kd->hqk', query_tile, key_window, preferred_element_type=...]
    another operation x1 -> x0, loops' own time: 25 us -> none  [attend(): return lax.map(one_tile, (query_tiles, offsets))]
    all_to_all x1 -> x0, blocking collectives: 23.3 us -> none  [on_device(): lax.all_to_all(output_region, 'dp', split_axis=0, concat_axis=1, tiled=True)]
    all_to_all x3 -> x0, waiting for transfers between devices: 22.4 us -> none  [the longest x1 15.1 us: on_device(): lax.all_to_all(key_copies, 'dp', split_axis=1, concat_axis=0, tiled=True)]
    all_to_all x3 -> x0, starting transfers between devices: 19.9 us -> none  [the longest x1 8.07 us: on_device(): lax.all_to_all(key_copies, 'dp', split_axis=1, concat_axis=0, tiled=True)]
    ppermute x2 -> x0, waiting for transfers between devices: 9.66 us -> none  [passed_along(): return lax.ppermute(block, axis, route)]
    ppermute x2 -> x0, starting transfers between devices: 9.51 us -> none  [passed_along(): return lax.ppermute(block, axis, route)]
  transfers between devices with their start and end apart: 5 -> 0, of which waited for: 3 -> 0; matrix products, arithmetic and copies ran while one was open for 3% -> 0% of each run, Pallas kernels for 0% -> 0%
where the time goes in v1:
time: 74.6 us; the launch traced here: 73.8 us
  Pallas kernels  69.1 us (93%)
  local copies, waits for them, and re-layouts  4.75 us (6%)
    pallas_call x1, Pallas kernels, on_device(): pl.pallas_call(kernel, out_shape=jax.ShapeDtypeStruct(queries.shape, jnp....  69.1 us
    unnamed x9, local copies, waits for them, and re-layouts  4.75 us

profile of v1, /device:TPU:99, one launch (start us, length us, event | category | flops | bytes accessed | tf_op | source)
XLA Modules:
  0.0 73.8 jit_solution(4857007166569436787)
XLA Ops:
  0.0 0.0 copy-start
  0.0 1.2 %copy-done = bf16[128,32,128]{2,1,0:T(8,128)(2,1)S(1)} copy-done((bf16[128,32,128]{2,1,0:T(8,128)(2,1)S(1)}, bf16[128,32,128]{2,1,0:T(8,128)(2,1)}, u32[]{:S(2)}) %copy-start) | copy-done | bytes 1048600
  1.2 0.0 copy-start.1
  1.2 0.9 %copy-done.1 = bf16[128,8,128]{2,1,0:T(8,128)(2,1)S(1)} copy-done((bf16[128,8,128]{2,1,0:T(8,128)(2,1)S(1)}, bf16[128,8,128]{2,1,0:T(8,128)(2,1)}, u32[]{:S(2)}) %copy-start.1) | copy-done | bytes 262168
  2.2 0.0 copy-start.2
  2.2 0.9 %copy-done.2 = bf16[128,8,128]{2,1,0:T(8,128)(2,1)S(1)} copy-done((bf16[128,8,128]{2,1,0:T(8,128)(2,1)S(1)}, bf16[128,8,128]{2,1,0:T(8,128)(2,1)}, u32[]{:S(2)}) %copy-start.2) | copy-done | bytes 262168
  3.1 0.0 copy-start.3
  3.1 0.7 copy-done.3
  3.8 69.1 %attend.1 = bf16[128,32,128]{2,1,0:T(8,128)(2,1)S(1)} custom-call(bf16[128,32,128]{2,1,0:T(8,128)(2,1)S(1)} %copy-done, bf16[128,8,128]{2,1,0:T(8,128)(2,1)S(1)} %copy-done.1, bf16[128,8,128]{2,1,0:T(8,128)(2,1)S(1)} %copy-done.2, s32[32]{0:T(128)S(1)} %copy-done.3), custom_call_target="tpu_custom_call" | custom-call | tf_op jit(solution)/shard_map/attend/pallas_call | solution.py:255
  72.8 1.0 %copy.6 = bf16[128,32,128]{2,1,0:T(8,128)(2,1)} copy(bf16[128,32,128]{2,1,0:T(8,128)(2,1)S(1)} %attend.1) | data formatting | bytes 2097152
Async XLA Ops:
  0.0 1.2 %copy-start = (bf16[128,32,128]{2,1,0:T(8,128)(2,1)S(1)}, bf16[128,32,128]{2,1,0:T(8,128)(2,1)}, u32[]{:S(2)}) copy-start(bf16[128,32,128]{2,1,0:T(8,128)(2,1)} %q_ref.1) | copy-start | bytes 3145732
  1.2 0.9 %copy-start.1 = (bf16[128,8,128]{2,1,0:T(8,128)(2,1)S(1)}, bf16[128,8,128]{2,1,0:T(8,128)(2,1)}, u32[]{:S(2)}) copy-start(bf16[128,8,128]{2,1,0:T(8,128)(2,1)} %k_ref.1) | copy-start | bytes 786436
  2.2 0.9 %copy-start.2 = (bf16[128,8,128]{2,1,0:T(8,128)(2,1)S(1)}, bf16[128,8,128]{2,1,0:T(8,128)(2,1)}, u32[]{:S(2)}) copy-start(bf16[128,8,128]{2,1,0:T(8,128)(2,1)} %v_ref.1) | copy-start | bytes 786436
  3.1 0.7 copy-start.3

commit v2 on v0

v2 whole, which is shorter than its diff:
```python
import jax
import jax.numpy as jnp
from jax import lax
from jax.experimental import pallas as pl
from jax.experimental.pallas import tpu as pltpu
from jax.sharding import PartitionSpec as P

STEPS = (
    (1114240, 2621984, 2097296, 6291600, 2162864, 4259968, 6358528, 6358528),
    (656384, 2294416, 6423568, 2163744, 2229248, 2228400, 6489632, 6422593),
    (2294016, 1459200, 2293888, 525360, 4260352, 2098224, 462931, 6488177),
    (721936, 1048752, 721056, 2294432, 332832, 332432, 299076, 278631),
    (5440800, 4326672, 278593, 720969, 299092, 409689, 540947, 540745),
    (2097225, 1704004, 1065049, 267280, 655764, 1196153, 344131, 274945),
    (364660, 345136, 398336, 430148, 1459248, 2293905, 1654873, 344145),
    (430736, 475440, 430180, 332036, 2293905, 4428825, 405764, 1654873),
    (266307, 364617, 4391204, 495700, 267273, 4194628, 430180, 2298151),
    (496160, 1065027, 1523825, 1454356, 397394, 1392705, 471204, 340228),
    (331875, 790633, 2162771, 463361, 364612, 398368, 475221, 430180),
    (2109569, 340089, 528739, 725348, 1388804, 463008, 1261689, 405924),
    (472073, 4231444, 4297265, 4231697, 2101380, 1409140, 1196181, 475218),
    (1261793, 331874, 4362401, 274804, 430193, 1540609, 737587, 737401),
    (4297233, 406553, 274505, 4362369, 524355, 671827, 4231729, 472073),
    (335940, 1261793, 495697, 364641, 496146, 299553, 4296801, 807961),
    (4362803, 4362771, 1393153, 4427921, 589939, 2297958, 336937, 1262633),
    (401492, 987251, 2232402, 606291, 475681, 1262601, 4428307, 479303),
    (2232579, 4428322, 479298, 1126947, 405832, 430194, 283139, 4428305),
    (410681, 295171, 4231512, 659525, 4297265, 4362307, 295029, 356449),
    (2170993, 360739, 426082, 270897, 528498, 270611, 557237, 2171080),
    (294983, 2367570, 4427847, 294997, 1258537, 528483, 487971, 413960),
    (2236707, 356659, 606504, 4296791, 282690, 282706, 1409089, 487896),
    (360533, 417896, 1077777, 487528, 1262649, 2302113, 332321, 348648),
    (426103, 807032, 741445, 401923, 352354, 413781, 1081704, 741880),
    (414003, 872519, 467045, 491784, 413857, 401585, 356422, 270406),
    (340088, 352326, 471112, 2232453, 2105521, 295029, 2171128, 401510),
    (352882, 422117, 286840, 1142898, 360565, 426099, 270648, 483414),
    (806999, 483573, 356437, 610407, 1147426, 483398, 417863, 114),
    (421990, 467063, 422006, 479528, 356456, 352327, 401511, 0),
    (286965, 0, 487510, 1273971, 491816, 421975, 544869, 0),
    (270454, 0, 102, 335960, 1142887, 119, 467062, 0),
    (0, 0, 0, 291128, 348472, 0, 86, 0),
    (0, 0, 0, 286821, 290886, 0, 0, 0),
    (0, 0, 0, 417878, 483623, 0, 0, 0),
    (0, 0, 0, 118, 487526, 0, 0, 0),
)
OPEN = (10, 5, 8, 8, 7, 7, 4, 2)
MOST = 12
PARTS = 4
BACK = 8
THROUGH = 9
DIRS = 4
BLK = 128
HD = 128
LOG2E = 1.4426950408889634
MASKED = -1e30
MESH = pl.DeviceIdType.MESH


def kernel(
    q_hbm, k_hbm, v_hbm, docs_hbm, o_ref,
    q_in, k_in, v_in, docs, parts, give_kv, give_q, give_out, qx, qf, kf, vf, qs, acc, top, even, odd,
    load_sem, send_sem, part_sem, kv_send, kv_sem, q_send, q_sem, out_send, out_sem,
):
    tokens, q_heads, _ = q_in.shape
    kv_heads = k_in.shape[1]
    group = q_heads // kv_heads
    rows = group * tokens
    dp = lax.axis_index("dp")
    z = lax.axis_index("ctx")
    planes = lax.axis_size("ctx")
    x, y, core = dp // 8, (dp // 2) % 4, dp % 2
    chip = dp // 2
    other = 1 - core

    def one_if(condition):
        return jnp.where(condition, jnp.int32(1), jnp.int32(0))

    def at(to_x, to_y, to_z, to_core):
        return ((to_x % 4) * 8 + (to_y % 4) * 2 + to_core, to_z)

    loads = [
        pltpu.make_async_copy(src, dst, load_sem.at[i])
        for i, (src, dst) in enumerate(((k_hbm, k_in), (v_hbm, v_in), (q_hbm, q_in), (docs_hbm, docs)))
    ]
    for load in loads:
        load.start()

    over_ahead = one_if(x == 3)
    over_beyond = one_if((x == 1) | (x == 2))
    has_ahead = z + over_ahead < planes
    has_behind = z - one_if(x == 0) >= 0
    has_beyond = z + over_beyond < planes
    has_beyond_from = z - one_if(x <= 1) >= 0
    has_through = z + one_if(x >= 2) < planes
    pair = at(x, y, z, other)
    up = at(x, y + 1, z, core)
    down = at(x, y + 3, z, core)
    ahead = at(x + 1, y, z + over_ahead, core)
    through = at(x + 3, y, z, core)

    barrier = pltpu.get_barrier_semaphore()

    def greet(device):
        pl.semaphore_signal(barrier, inc=1, device_id=device, device_id_type=MESH)

    for friend in (pair, up, down, through, at(x + 1, y, z, core)):
        greet(friend)
    maybe = (
        (has_ahead, ahead),
        (has_behind, at(x + 3, y, z - one_if(x == 0), core)),
        (has_beyond, at(x + 3, y, z + over_beyond, core)),
        (has_beyond_from, at(x + 1, y, z - one_if(x <= 1), core)),
    )
    greeted = jnp.int32(5)
    for there, friend in maybe:
        greeted = greeted + one_if(there)
        pl.when(there)(lambda friend=friend: greet(friend))

    loads[0].wait()
    kf[...] = k_in[...].astype(jnp.float32).reshape(tokens * kv_heads, HD)
    loads[1].wait()
    vf[...] = v_in[...].astype(jnp.float32).reshape(tokens * kv_heads, HD)
    mine = pl.multiple_of(core * 2 * BLK, 2 * BLK)
    for p in range(PARTS):
        head = pl.ds(other * PARTS + p, tokens, stride=kv_heads)
        give_kv[p, pl.ds(0, BLK), :] = kf[head, :].astype(jnp.bfloat16)
        give_kv[p, pl.ds(BLK, BLK), :] = vf[head, :].T.astype(jnp.bfloat16)
    for p in range(PARTS):
        head = pl.ds(core * PARTS + p, tokens, stride=kv_heads)
        parts[p, pl.ds(mine, BLK), :] = kf[head, :].astype(jnp.bfloat16)
        parts[p, pl.ds(mine + BLK, BLK), :] = vf[head, :].T.astype(jnp.bfloat16)

    pl.semaphore_wait(barrier, greeted)

    def send(src, dst, sem, landed, device):
        pltpu.make_async_remote_copy(
            src_ref=src, dst_ref=dst, send_sem=sem, recv_sem=landed, device_id=device, device_id_type=MESH
        ).start()

    def await_copy(ref, sem):
        pltpu.make_async_copy(ref, ref, sem).wait()

    for p in range(PARTS):
        send(give_kv.at[p], parts.at[p, pl.ds(mine, 2 * BLK)], kv_send, kv_sem.at[p], pair)

    loads[2].wait()
    qf[...] = q_in[...].astype(jnp.float32).reshape(tokens * q_heads, HD)

    def queries_of(p, r, side):
        return qf[pl.ds((side * PARTS + p) * group + r, tokens, stride=q_heads), :].T

    for p in range(PARTS):
        for r in range(group):
            give_q[p, :, pl.ds(r * tokens, tokens)] = queries_of(p, r, other).astype(jnp.bfloat16)
        send(give_q.at[p], qx.at[p], q_send, q_sem.at[p], pair)

    scale = LOG2E * HD**-0.5

    def put_queries(p, at_rows, value):
        scaled = value * scale
        high = scaled.astype(jnp.bfloat16)
        qs[p, pl.ds(0, HD), at_rows] = high
        qs[p, pl.ds(HD, HD), at_rows] = (scaled - high.astype(jnp.float32)).astype(jnp.bfloat16)

    for p in range(PARTS):
        for r in range(group):
            put_queries(p, pl.ds(pl.multiple_of(core * rows + r * tokens, tokens), tokens), queries_of(p, r, core))

    loads[3].wait()
    reach = []
    for b in range(2):
        block = (z * 16 + chip) * 2 + b
        end = jnp.int32(0)
        start = jnp.int32(0)
        for i in range(docs.shape[0]):
            end = end + docs[i]
            start = jnp.where(end <= block, end, start)
        reach.append(block - start)

    def bias_of(back, b):
        return jnp.where(back <= reach[b], jnp.float32(0), jnp.float32(MASKED))

    ones = jnp.ones((16, 2 * BLK), jnp.bfloat16)

    def score(slot, p, into):
        keys = jnp.concatenate([parts[slot, pl.ds(0, BLK), :], parts[slot, pl.ds(2 * BLK, BLK), :]], axis=0)
        keys = jnp.concatenate([keys, keys], axis=1)
        for b in range(2):
            at_rows = pl.ds(b * rows, rows)
            into[:, at_rows] = jnp.dot(keys, qs[p, :, at_rows], preferred_element_type=jnp.float32)

    def combine(slot, p, scores, biases, causal=None):
        values = jnp.concatenate([parts[slot, pl.ds(BLK, BLK), :], parts[slot, pl.ds(3 * BLK, BLK), :]], axis=1)
        values = jnp.concatenate([values, ones], axis=0)
        for b in range(2):
            at_rows = pl.ds(b * rows, rows)
            halves = [scores[pl.ds(h * BLK, BLK), at_rows] for h in range(2)]
            if causal is not None:
                halves[b] = halves[b] + causal
            peaks = [jnp.max(halves[h], axis=0, keepdims=True) + biases[b][h] for h in range(2)]
            new_top = jnp.maximum(peaks[0], peaks[1])
            if causal is None:
                old_top = top[p, pl.ds(0, 1), at_rows]
                new_top = jnp.maximum(old_top, new_top)
            weights = [jnp.exp2(halves[h] - (new_top - biases[b][h])).astype(jnp.bfloat16) for h in range(2)]
            summed = jnp.dot(values, jnp.concatenate(weights, axis=0), preferred_element_type=jnp.float32)
            if causal is None:
                acc[p, :, at_rows] = acc[p, :, at_rows] * jnp.exp2(old_top - new_top) + summed
            else:
                acc[p, :, at_rows] = summed
            top[p, pl.ds(0, 1), at_rows] = new_top

    def combine_back(k, p, scores):
        biases = [[bias_of(2 * k + b - h, b) for h in range(2)] for b in range(2)]
        combine(k * PARTS + p, p, scores, biases)

    shifts = (
        jnp.where(y == 3, jnp.int32(-3), jnp.int32(1)),
        jnp.where(y == 0, jnp.int32(3), jnp.int32(-1)),
        jnp.int32(4),
    )
    targets = (up, down, ahead)
    allowed = (True, True, has_ahead)

    def of_place(entry):
        value = jnp.int32(entry[7])
        for j in range(7):
            value = jnp.where(y * 2 + core == j, jnp.int32(entry[j]), value)
        return value

    def word_at(index):
        value = jnp.int32(0)
        for i, entry in enumerate(STEPS):
            value = jnp.where(index == i, of_place(entry), value)
        return value

    def step(s, counts):
        code = (word_at(s // 2) >> (12 * (s % 2))) % 4096
        k, p, waits, bits = code % 16, (code // 16) % 4, (code // 64) % 2, code // 128
        slot = k * PARTS + p
        here = (k == 0) | ((k == THROUGH) & has_beyond) | ((k != THROUGH) & ((z > 0) | (chip >= k)))

        @pl.when(here & (waits == 1))
        def _():
            await_copy(parts.at[slot], part_sem.at[slot])

        new_counts = []
        for d in range(3):
            go = here & ((bits >> d) % 2 == 1) & allowed[d]
            new_counts.append(counts[d] + one_if(go))

            @pl.when(go)
            def _():
                to = slot + shifts[d] * PARTS
                send(parts.at[slot], parts.at[to], send_sem.at[d], part_sem.at[to], targets[d])

        go = here & (bits // 8 == 1) & ((k == THROUGH) | has_through)
        new_counts.append(counts[3] + one_if(go))

        @pl.when(go)
        def _():
            to = jnp.where(k == THROUGH, BACK * PARTS + p, THROUGH * PARTS + p)
            device = at(x + 3, y, z + jnp.where(k == THROUGH, over_beyond, 0), core)
            send(parts.at[slot], parts.at[to], send_sem.at[3], part_sem.at[to], device)

        done, before_k, before_p = counts[4:]
        go = here & (waits == 1) & (k != THROUGH)

        @pl.when(go & (done == 0))
        def _():
            score(slot, p, even)

        @pl.when(go & (done % 2 == 1))
        def _():
            score(slot, p, odd)
            combine_back(before_k, before_p, even)

        @pl.when(go & (done > 0) & (done % 2 == 0))
        def _():
            score(slot, p, even)
            combine_back(before_k, before_p, odd)

        new_counts += [done + one_if(go), jnp.where(go, k, before_k), jnp.where(go, p, before_p)]
        return tuple(new_counts)

    for p in range(PARTS):
        await_copy(give_kv.at[p], kv_sem.at[p])

    def attend_own():
        key = lax.broadcasted_iota(jnp.int32, (BLK, rows), 0)
        query = lax.broadcasted_iota(jnp.int32, (BLK, rows), 1) % tokens
        causal = jnp.where(key <= query, jnp.float32(0), jnp.float32(MASKED))
        biases = [[jnp.float32(0), jnp.float32(MASKED)], [bias_of(1, 1), jnp.float32(0)]]
        for p in range(PARTS):
            await_copy(qx.at[p], q_sem.at[p])
            put_queries(p, pl.ds(pl.multiple_of(other * rows, rows), rows), qx[p].astype(jnp.float32))
        score(0, 0, even)
        for p in range(PARTS):
            if p + 1 < PARTS:
                score(p + 1, p + 1, (even, odd)[(p + 1) % 2])
            combine(p, p, (even, odd)[p % 2], biases, causal)

    zero = jnp.int32(0)
    opening = of_place(OPEN)
    state = lax.fori_loop(0, opening, step, (zero,) * 7)
    attend_own()
    state = lax.fori_loop(opening, 2 * len(STEPS), step, state)
    counts, (done, before_k, before_p) = state[:4], state[4:]
    for odd_last in range(2):
        @pl.when((done > 0) & (done % 2 == 1 - odd_last))
        def _():
            combine_back(before_k, before_p, (even, odd)[odd_last])

    def result(p, r, side):
        at_rows = pl.ds(pl.multiple_of(side * rows + r * tokens, tokens), tokens)
        return (acc[p, pl.ds(0, HD), at_rows] / acc[p, pl.ds(HD, 1), at_rows]).T.astype(jnp.bfloat16)

    for p in range(PARTS):
        for r in range(group):
            give_out[p, pl.ds(r * tokens, tokens), :] = result(p, r, other)
        send(give_out.at[p], o_ref.at[core * PARTS + p], out_send, out_sem, pair)
    for p in range(PARTS):
        for r in range(group):
            o_ref[core * PARTS + p, pl.ds(r * tokens, tokens), :] = result(p, r, core)

    for d in range(DIRS):
        for n in range(1, MOST + 1):
            @pl.when(counts[d] == n)
            def _():
                await_copy(parts.at[pl.ds(0, n)], send_sem.at[d])
    await_copy(give_kv, kv_send)
    await_copy(give_q, q_send)
    await_copy(give_out, out_send)
    await_copy(give_out, out_sem)


def on_device(queries, keys, values, doc_blocks):
    tokens, q_heads, _ = queries.shape
    kv_heads = keys.shape[1]
    group = q_heads // kv_heads
    rows = group * tokens
    bf16, f32 = jnp.bfloat16, jnp.float32
    anywhere = pl.BlockSpec(memory_space=pl.ANY)
    dma = pltpu.SemaphoreType.DMA
    by_head = pl.pallas_call(
        kernel,
        out_shape=jax.ShapeDtypeStruct((kv_heads, rows, HD), bf16),
        in_specs=[anywhere] * 4,
        out_specs=pl.BlockSpec(memory_space=pltpu.VMEM),
        scratch_shapes=[
            pltpu.VMEM(queries.shape, bf16),
            pltpu.VMEM(keys.shape, bf16),
            pltpu.VMEM(values.shape, bf16),
            pltpu.SMEM(doc_blocks.shape, jnp.int32),
            pltpu.VMEM(((THROUGH + 1) * PARTS, 4 * BLK, HD), bf16),
            pltpu.VMEM((PARTS, 2 * BLK, HD), bf16),
            pltpu.VMEM((PARTS, HD, rows), bf16),
            pltpu.VMEM((PARTS, rows, HD), bf16),
            pltpu.VMEM((PARTS, HD, rows), bf16),
            pltpu.VMEM((tokens * q_heads, HD), f32),
            pltpu.VMEM((tokens * kv_heads, HD), f32),
            pltpu.VMEM((tokens * kv_heads, HD), f32),
            pltpu.VMEM((PARTS, 2 * HD, 2 * rows), bf16),
            pltpu.VMEM((PARTS, HD + 16, 2 * rows), f32),
            pltpu.VMEM((PARTS, 8, 2 * rows), f32),
            pltpu.VMEM((2 * BLK, 2 * rows), f32),
            pltpu.VMEM((2 * BLK, 2 * rows), f32),
            dma((4,)),
            dma((DIRS,)),
            dma(((THROUGH + 1) * PARTS,)),
            dma,
            dma((PARTS,)),
            dma,
            dma((PARTS,)),
            dma,
            dma,
        ],
        compiler_params=pltpu.CompilerParams(
            collective_id=0, has_side_effects=True, vmem_limit_bytes=63 << 20
        ),
        name="attend",
    )(queries, keys, values, doc_blocks)
    by_head = by_head.reshape(q_heads, tokens, HD)
    return jnp.transpose(by_head, (1, 0, 2))


def solution(mesh):
    placed = P(("ctx", "dp"), None, None)
    return jax.shard_map(
        on_device,
        mesh=mesh,
        in_specs=(placed, placed, placed, P()),
        out_specs=placed,
        check_vma=False,
    )
```

time: 180 us -> 57.8 us (0.32)
  the two profiles are of different devices: /device:TPU:99 before, /device:TPU:201 now
where the time goes in v2:
time: 57.8 us; the launch traced here: 57.7 us
  Pallas kernels  54.8 us (95%)
  local copies, waits for them, and re-layouts  2.87 us (5%)
    pallas_call x1, Pallas kernels, on_device(): pl.pallas_call(kernel, out_shape=jax.ShapeDtypeStruct((kv_heads, rows, HD...  54.8 us
    reshape x1, local copies, waits for them, and re-layouts, on_device(): by_head = by_head.reshape(q_heads, tokens, HD)  2.87 us

profile of v2, /device:TPU:201, one launch (start us, length us, event | category | flops | bytes accessed | tf_op | source)
XLA Modules:
  0.0 57.7 jit_solution(1491131263475612171)
XLA Ops:
  0.0 54.8 %attend.1 = bf16[8,512,128]{2,1,0:T(8,128)(2,1)} custom-call(bf16[128,32,128]{2,1,0:T(8,128)(2,1)} %q_hbm.1, bf16[128,8,128]{2,1,0:T(8,128)(2,1)} %k_hbm.1, bf16[128,8,128]{2,1,0:T(8,128)(2,1)} %v_hbm.1, s32[32]{0:T(128)} %docs_hbm.1), custom_call_target="tpu_custom_call" | custom-call | tf_op jit(solution)/shard_map/attend/pallas_call | solution.py:345
  54.8 2.9 %copy.7 = bf16[32,128,128]{2,0,1:T(8,128)(2,1)} copy(bf16[32,128,128]{2,1,0:T(8,128)(2,1)} %bitcast.4) | data formatting | bytes 2097152 | tf_op jit(solution)/shard_map/reshape | solution.py:383

commit v3 on v2

--- a/solution.py
+++ b/solution.py
@@ -6,49 +6,83 @@
 from jax.sharding import PartitionSpec as P
 
 STEPS = (
-    (1114240, 2621984, 2097296, 6291600, 2162864, 4259968, 6358528, 6358528),
-    (656384, 2294416, 6423568, 2163744, 2229248, 2228400, 6489632, 6422593),
-    (2294016, 1459200, 2293888, 525360, 4260352, 2098224, 462931, 6488177),
-    (721936, 1048752, 721056, 2294432, 332832, 332432, 299076, 278631),
-    (5440800, 4326672, 278593, 720969, 299092, 409689, 540947, 540745),
-    (2097225, 1704004, 1065049, 267280, 655764, 1196153, 344131, 274945),
-    (364660, 345136, 398336, 430148, 1459248, 2293905, 1654873, 344145),
-    (430736, 475440, 430180, 332036, 2293905, 4428825, 405764, 1654873),
-    (266307, 364617, 4391204, 495700, 267273, 4194628, 430180, 2298151),
-    (496160, 1065027, 1523825, 1454356, 397394, 1392705, 471204, 340228),
-    (331875, 790633, 2162771, 463361, 364612, 398368, 475221, 430180),
-    (2109569, 340089, 528739, 725348, 1388804, 463008, 1261689, 405924),
-    (472073, 4231444, 4297265, 4231697, 2101380, 1409140, 1196181, 475218),
-    (1261793, 331874, 4362401, 274804, 430193, 1540609, 737587, 737401),
-    (4297233, 406553, 274505, 4362369, 524355, 671827, 4231729, 472073),
-    (335940, 1261793, 495697, 364641, 496146, 299553, 4296801, 807961),
-    (4362803, 4362771, 1393153, 4427921, 589939, 2297958, 336937, 1262633),
-    (401492, 987251, 2232402, 606291, 475681, 1262601, 4428307, 479303),
-    (2232579, 4428322, 479298, 1126947, 405832, 430194, 283139, 4428305),
-    (410681, 295171, 4231512, 659525, 4297265, 4362307, 295029, 356449),
-    (2170993, 360739, 426082, 270897, 528498, 270611, 557237, 2171080),
-    (294983, 2367570, 4427847, 294997, 1258537, 528483, 487971, 413960),
-    (2236707, 356659, 606504, 4296791, 282690, 282706, 1409089, 487896),
-    (360533, 417896, 1077777, 487528, 1262649, 2302113, 332321, 348648),
-    (426103, 807032, 741445, 401923, 352354, 413781, 1081704, 741880),
-    (414003, 872519, 467045, 491784, 413857, 401585, 356422, 270406),
-    (340088, 352326, 471112, 2232453, 2105521, 295029, 2171128, 401510),
-    (352882, 422117, 286840, 1142898, 360565, 426099, 270648, 483414),
-    (806999, 483573, 356437, 610407, 1147426, 483398, 417863, 114),
-    (421990, 467063, 422006, 479528, 356456, 352327, 401511, 0),
-    (286965, 0, 487510, 1273971, 491816, 421975, 544869, 0),
-    (270454, 0, 102, 335960, 1142887, 119, 467062, 0),
-    (0, 0, 0, 291128, 348472, 0, 86, 0),
-    (0, 0, 0, 286821, 290886, 0, 0, 0),
-    (0, 0, 0, 417878, 483623, 0, 0, 0),
-    (0, 0, 0, 118, 487526, 0, 0, 0),
+    (1073281, 1056899, 5243009, 1065091, 1073281, 1065089, 4194817, 4211201),
+    (2113792, 6316288, 8398339, 4219392, 4219392, 4219392, 4211715, 8406019),
+    (4211200, 8414720, 4210819, 12592128, 8397826, 8397824, 663621, 844288),
+    (14705664, 1065729, 656384, 655488, 1049090, 9462274, 3285095, 565329),
+    (1049601, 680961, 565351, 2228324, 656387, 581712, 2721831, 1189927),
+    (819280, 6307940, 4235536, 4212772, 835653, 2228324, 655875, 4219212),
+    (2229250, 8405139, 1091623, 827521, 17088784, 5302308, 3276871, 575590),
+    (843906, 655463, 827463, 17080403, 1180161, 680037, 4235342, 2744786),
+    (17072210, 2230308, 17080659, 2720531, 557157, 2252870, 1720675, 811525),
+    (2105490, 1614412, 4251778, 582097, 2728275, 1099813, 4251727, 1704007),
+    (4760140, 1712229, 671812, 713295, 17080837, 672072, 688398, 2228301),
+    (2244709, 17096972, 2244708, 1237074, 843909, 843844, 1212499, 680454),
+    (649255, 671814, 8405508, 565519, 581714, 4227346, 4325523, 1204299),
+    (836292, 17080422, 647303, 557714, 590098, 8405120, 598290, 2383950),
+    (2222117, 2236550, 2910244, 598115, 4325508, 565344, 557269, 696848),
+    (574030, 557640, 1196559, 786706, 600103, 17096992, 2253321, 1220682),
+    (680149, 17088786, 622945, 5316678, 663650, 2891920, 589911, 2203740),
+    (2269702, 4825234, 1763430, 2383950, 622882, 4817028, 4259991, 4333666),
+    (4786214, 647751, 4784462, 696415, 1106441, 745574, 4317276, 2326742),
+    (2211932, 2203783, 696390, 1220705, 795140, 641062, 1777741, 1835527),
+    (786631, 1081929, 598366, 2351620, 696390, 1269847, 770401, 4284693),
+    (2703879, 786524, 704863, 802890, 778513, 688203, 614621, 1843470),
+    (778313, 1122890, 688224, 1753610, 1065480, 2850901, 745568, 4276292),
+    (688342, 720995, 729186, 2376206, 729375, 811141, 720966, 688216),
+    (4268131, 794699, 720973, 5857497, 606732, 704607, 704602, 589917),
+    (762134, 639069, 614491, 3883100, 4251801, 598114, 606303, 778334),
+    (770264, 712802, 737373, 688221, 639265, 729165, 98, 729175),
+    (802913, 688223, 606289, 770136, 1098250, 737368, 0, 745545),
+    (614490, 745561, 92, 745544, 786709, 761937, 0, 90),
+    (630875, 770133, 0, 77, 811534, 606287, 0, 0),
+    (663639, 704602, 0, 0, 2211915, 94, 0, 0),
+    (89, 0, 0, 0, 704596, 0, 0, 0),
+    (0, 0, 0, 0, 745560, 0, 0, 0),
+    (0, 0, 0, 0, 647260, 0, 0, 0),
+    (0, 0, 0, 0, 737367, 0, 0, 0),
+    (0, 0, 0, 0, 761950, 0, 0, 0),
 )
-OPEN = (10, 5, 8, 8, 7, 7, 4, 2)
-MOST = 12
+UNITS = (
+    (720, 659, 528, 528, 656, 592, 325, 465),
+    (1106, 1040, 645, 979, 709, 647, 401, 517),
+    (1356, 1228, 967, 1164, 1156, 1043, 652, 716),
+    (1413, 1285, 1107, 1233, 1235, 1094, 784, 902),
+    (1679, 1425, 1348, 1287, 1293, 1352, 839, 978),
+    (1732, 1606, 1426, 1359, 1618, 1426, 974, 1039),
+    (1998, 1682, 1807, 1431, 1671, 1476, 1123, 1187),
+    (2054, 1992, 1955, 1490, 1800, 1888, 1170, 1223),
+    (2133, 2052, 2145, 1669, 2057, 1925, 1231, 1296),
+    (2195, 2317, 2188, 1796, 2146, 2209, 1428, 1357),
+    (2440, 2375, 2327, 1891, 2193, 2316, 1491, 1555),
+    (2524, 2447, 2382, 1929, 2316, 2459, 1801, 1611),
+    (2631, 2633, 2440, 2080, 2593, 2574, 1877, 1742),
+    (2720, 2780, 2502, 2118, 2630, 2647, 1924, 1941),
+    (2826, 2848, 2581, 2254, 2709, 2763, 2135, 1994),
+    (2889, 2890, 2654, 2399, 2847, 2836, 2184, 2140),
+    (2975, 3043, 2697, 2453, 3097, 2901, 2396, 2274),
+    (3030, 3096, 2783, 2529, 3210, 2972, 2509, 2390),
+    (3092, 3147, 2838, 2762, 3470, 3107, 2585, 2592),
+    (3171, 3233, 2912, 2850, 3744, 3167, 2657, 2849),
+    (3357, 3293, 2964, 2966, 3875, 3222, 2718, 2884),
+    (3416, 3342, 3042, 3161, 3915, 3298, 2781, 3032),
+    (3486, 3426, 3097, 3211, 4052, 3337, 2827, 3092),
+    (3553, 3479, 3149, 3292, 4118, 3405, 2912, 3165),
+    (3618, 3551, 3224, 3354, 4184, 3481, 2971, 3208),
+    (3674, 3604, 3291, 3421, 4251, 3544, 3014, 3294),
+    (3723, 3673, 3339, 3476, 4316, 3610, 3096, 3359),
+    (3803, 3739, 3421, 3544, 4367, 3665, 3162, 3415),
+    (3853, 3797, 3482, 3614, 4439, 3741, 3222, 3481),
+    (3927, 3870, 3537, 3656, 4506, 3791, 3295, 3529),
+    (3985, 3930, 3594, 3739, 4574, 3850, 3338, 3611),
+    (4057, 3990, 3676, 3789, 4637, 3934, 3426, 3674),
+)
+OPEN = (10, 9, 7, 7, 9, 8, 4, 5)
+MOST = 13
 PARTS = 4
 BACK = 8
 THROUGH = 9
-DIRS = 4
+DIRS = 5
 BLK = 128
 HD = 128
 LOG2E = 1.4426950408889634
@@ -98,6 +132,13 @@
     ahead = at(x + 1, y, z + over_ahead, core)
     through = at(x + 3, y, z, core)
 
+    last_here = PARTS * jnp.where(z > 0, jnp.int32(BACK), jnp.minimum(chip, BACK)) + PARTS - 1
+
+    def clear(slot, c):
+        parts[slot] = jnp.zeros((4 * BLK, HD), jnp.bfloat16)
+        return c
+    lax.fori_loop(last_here + 1, (BACK + 1) * PARTS, clear, 0)
+
     barrier = pltpu.get_barrier_semaphore()
 
     def greet(device):
@@ -115,6 +156,23 @@
     for there, friend in maybe:
         greeted = greeted + one_if(there)
         pl.when(there)(lambda friend=friend: greet(friend))
+
+    def of_place(entry):
+        pairs = [jnp.where(core == 0, jnp.int32(entry[2 * i]), jnp.int32(entry[2 * i + 1])) for i in range(4)]
+        return jnp.where(y < 2, jnp.where(y == 0, pairs[0], pairs[1]), jnp.where(y == 2, pairs[2], pairs[3]))
+
+    steps = [of_place(entry) for entry in STEPS]
+    units = [of_place(entry) for entry in UNITS]
+
+    def pick(values, index):
+        while len(values) > 1:
+            low = (index & 1) == 0
+            values = [
+                jnp.where(low, values[i], values[i + 1]) if i + 1 < len(values) else values[i]
+                for i in range(0, len(values), 2)
+            ]
+            index = index >> 1
+        return values[0]
 
     loads[0].wait()
     kf[...] = k_in[...].astype(jnp.float32).reshape(tokens * kv_heads, HD)
@@ -210,78 +268,49 @@
                 acc[p, :, at_rows] = summed
             top[p, pl.ds(0, 1), at_rows] = new_top
 
-    def combine_back(k, p, scores):
+    def combine_back(code, scores):
+        k, p = code >> 2, code & (PARTS - 1)
         biases = [[bias_of(2 * k + b - h, b) for h in range(2)] for b in range(2)]
-        combine(k * PARTS + p, p, scores, biases)
+        combine(code & 63, p, scores, biases)
 
     shifts = (
-        jnp.where(y == 3, jnp.int32(-3), jnp.int32(1)),
-        jnp.where(y == 0, jnp.int32(3), jnp.int32(-1)),
-        jnp.int32(4),
+        PARTS * jnp.where(y == 3, jnp.int32(-3), jnp.int32(1)),
+        PARTS * jnp.where(y == 0, jnp.int32(3), jnp.int32(-1)),
+        4 * PARTS,
+        THROUGH * PARTS,
+        (BACK - THROUGH) * PARTS,
     )
-    targets = (up, down, ahead)
-    allowed = (True, True, has_ahead)
-
-    def of_place(entry):
-        value = jnp.int32(entry[7])
-        for j in range(7):
-            value = jnp.where(y * 2 + core == j, jnp.int32(entry[j]), value)
-        return value
-
-    def word_at(index):
-        value = jnp.int32(0)
-        for i, entry in enumerate(STEPS):
-            value = jnp.where(index == i, of_place(entry), value)
-        return value
-
-    def step(s, counts):
-        code = (word_at(s // 2) >> (12 * (s % 2))) % 4096
-        k, p, waits, bits = code % 16, (code // 16) % 4, (code // 64) % 2, code // 128
-        slot = k * PARTS + p
-        here = (k == 0) | ((k == THROUGH) & has_beyond) | ((k != THROUGH) & ((z > 0) | (chip >= k)))
-
-        @pl.when(here & (waits == 1))
+    targets = (up, down, ahead, through, at(x + 3, y, z + over_beyond, core))
+    open_ways = 3 + 4 * one_if(has_ahead) + 8 * one_if(has_through) + 16 * one_if(has_beyond)
+
+    def step(s, sent):
+        word = pick(steps, s >> 1) >> (13 * (s & 1))
+        slot = word & 63
+        here = (slot <= last_here) | ((slot >= THROUGH * PARTS) & has_beyond)
+        ways = jnp.where(here, (word >> 7) & open_ways, 0)
+
+        @pl.when(here & ((word & 64) != 0))
         def _():
             await_copy(parts.at[slot], part_sem.at[slot])
 
-        new_counts = []
-        for d in range(3):
-            go = here & ((bits >> d) % 2 == 1) & allowed[d]
-            new_counts.append(counts[d] + one_if(go))
-
-            @pl.when(go)
-            def _():
-                to = slot + shifts[d] * PARTS
-                send(parts.at[slot], parts.at[to], send_sem.at[d], part_sem.at[to], targets[d])
-
-        go = here & (bits // 8 == 1) & ((k == THROUGH) | has_through)
-        new_counts.append(counts[3] + one_if(go))
-
-        @pl.when(go)
+        @pl.when(ways != 0)
         def _():
-            to = jnp.where(k == THROUGH, BACK * PARTS + p, THROUGH * PARTS + p)
-            device = at(x + 3, y, z + jnp.where(k == THROUGH, over_beyond, 0), core)
-            send(parts.at[slot], parts.at[to], send_sem.at[3], part_sem.at[to], device)
-
-        done, before_k, before_p = counts[4:]
-        go = here & (waits == 1) & (k != THROUGH)
-
-        @pl.when(go & (done == 0))
-        def _():
-            score(slot, p, even)
-
-        @pl.when(go & (done % 2 == 1))
-        def _():
-            score(slot, p, odd)
-            combine_back(before_k, before_p, even)
-
-        @pl.when(go & (done > 0) & (done % 2 == 0))
-        def _():
-            score(slot, p, even)
-            combine_back(before_k, before_p, odd)
-
-        new_counts += [done + one_if(go), jnp.where(go, k, before_k), jnp.where(go, p, before_p)]
-        return tuple(new_counts)
+            for d in range(DIRS):
+                @pl.when((ways & (1 << d)) != 0)
+                def _():
+                    to = slot + shifts[d]
+                    send(parts.at[slot], parts.at[to], send_sem.at[d], part_sem.at[to], targets[d])
+        for d in range(DIRS):
+            sent = sent + (((ways >> d) & 1) << (5 * d))
+        return sent
+
+    def unit(u, now, sent, before, scores, scores_before):
+        word = pick(units, u)
+        slot, end = word & 63, word >> 6
+        sent = lax.fori_loop(now, end, step, sent)
+        score(slot, slot & (PARTS - 1), scores)
+        combine_back(before, scores_before)
+        return end, sent, slot
 
     for p in range(PARTS):
         await_copy(give_kv.at[p], kv_sem.at[p])
@@ -300,16 +329,16 @@
                 score(p + 1, p + 1, (even, odd)[(p + 1) % 2])
             combine(p, p, (even, odd)[p % 2], biases, causal)
 
-    zero = jnp.int32(0)
     opening = of_place(OPEN)
-    state = lax.fori_loop(0, opening, step, (zero,) * 7)
+    sent = lax.fori_loop(0, opening, step, jnp.int32(0))
     attend_own()
-    state = lax.fori_loop(opening, 2 * len(STEPS), step, state)
-    counts, (done, before_k, before_p) = state[:4], state[4:]
-    for odd_last in range(2):
-        @pl.when((done > 0) & (done % 2 == 1 - odd_last))
-        def _():
-            combine_back(before_k, before_p, (even, odd)[odd_last])
+
+    def two_units(i, state):
+        state = unit(2 * i, *state, even, odd)
+        return unit(2 * i + 1, *state, odd, even)
+
+    _, sent, before = lax.fori_loop(0, len(UNITS) // 2, two_units, (opening, sent, jnp.int32(256)))
+    combine_back(before, odd)
 
     def result(p, r, side):
         at_rows = pl.ds(pl.multiple_of(side * rows + r * tokens, tokens), tokens)
@@ -325,7 +354,7 @@
 
     for d in range(DIRS):
         for n in range(1, MOST + 1):
-            @pl.when(counts[d] == n)
+            @pl.when(((sent >> (5 * d)) & 31) == n)
             def _():
                 await_copy(parts.at[pl.ds(0, n)], send_sem.at[d])
     await_copy(give_kv, kv_send)

time: 57.8 us -> 53.9 us (0.933)
  the two profiles are of different devices: /device:TPU:201 before, /device:TPU:99 now
where the time goes in v3:
time: 53.9 us; the launch traced here: 53.8 us
  Pallas kernels  50.9 us (94%)
  local copies, waits for them, and re-layouts  2.87 us (5%)
    pallas_call x1, Pallas kernels, on_device(): pl.pallas_call(kernel, out_shape=jax.ShapeDtypeStruct((kv_heads, rows, HD...  50.9 us
    reshape x1, local copies, waits for them, and re-layouts, on_device(): by_head = by_head.reshape(q_heads, tokens, HD)  2.87 us

profile of v3, /device:TPU:99, one launch (start us, length us, event | category | flops | bytes accessed | tf_op | source)
XLA Modules:
  0.0 53.8 jit_solution(3207755764894992124)
XLA Ops:
  0.0 50.9 %attend.1 = bf16[8,512,128]{2,1,0:T(8,128)(2,1)} custom-call(bf16[128,32,128]{2,1,0:T(8,128)(2,1)} %q_hbm.1, bf16[128,8,128]{2,1,0:T(8,128)(2,1)} %k_hbm.1, bf16[128,8,128]{2,1,0:T(8,128)(2,1)} %v_hbm.1, s32[32]{0:T(128)} %docs_hbm.1), custom_call_target="tpu_custom_call" | custom-call | tf_op jit(solution)/shard_map/attend/pallas_call | solution.py:374
  50.9 2.9 %copy.7 = bf16[32,128,128]{2,0,1:T(8,128)(2,1)} copy(bf16[32,128,128]{2,1,0:T(8,128)(2,1)} %bitcast.4) | data formatting | bytes 2097152 | tf_op jit(solution)/shard_map/reshape | solution.py:412

commit v4 on v3

--- a/solution.py
+++ b/solution.py
@@ -6,79 +6,98 @@
 from jax.sharding import PartitionSpec as P
 
 STEPS = (
-    (1073281, 1056899, 5243009, 1065091, 1073281, 1065089, 4194817, 4211201),
-    (2113792, 6316288, 8398339, 4219392, 4219392, 4219392, 4211715, 8406019),
-    (4211200, 8414720, 4210819, 12592128, 8397826, 8397824, 663621, 844288),
-    (14705664, 1065729, 656384, 655488, 1049090, 9462274, 3285095, 565329),
-    (1049601, 680961, 565351, 2228324, 656387, 581712, 2721831, 1189927),
-    (819280, 6307940, 4235536, 4212772, 835653, 2228324, 655875, 4219212),
-    (2229250, 8405139, 1091623, 827521, 17088784, 5302308, 3276871, 575590),
-    (843906, 655463, 827463, 17080403, 1180161, 680037, 4235342, 2744786),
-    (17072210, 2230308, 17080659, 2720531, 557157, 2252870, 1720675, 811525),
-    (2105490, 1614412, 4251778, 582097, 2728275, 1099813, 4251727, 1704007),
-    (4760140, 1712229, 671812, 713295, 17080837, 672072, 688398, 2228301),
-    (2244709, 17096972, 2244708, 1237074, 843909, 843844, 1212499, 680454),
-    (649255, 671814, 8405508, 565519, 581714, 4227346, 4325523, 1204299),
-    (836292, 17080422, 647303, 557714, 590098, 8405120, 598290, 2383950),
-    (2222117, 2236550, 2910244, 598115, 4325508, 565344, 557269, 696848),
-    (574030, 557640, 1196559, 786706, 600103, 17096992, 2253321, 1220682),
-    (680149, 17088786, 622945, 5316678, 663650, 2891920, 589911, 2203740),
-    (2269702, 4825234, 1763430, 2383950, 622882, 4817028, 4259991, 4333666),
-    (4786214, 647751, 4784462, 696415, 1106441, 745574, 4317276, 2326742),
-    (2211932, 2203783, 696390, 1220705, 795140, 641062, 1777741, 1835527),
-    (786631, 1081929, 598366, 2351620, 696390, 1269847, 770401, 4284693),
-    (2703879, 786524, 704863, 802890, 778513, 688203, 614621, 1843470),
-    (778313, 1122890, 688224, 1753610, 1065480, 2850901, 745568, 4276292),
-    (688342, 720995, 729186, 2376206, 729375, 811141, 720966, 688216),
-    (4268131, 794699, 720973, 5857497, 606732, 704607, 704602, 589917),
-    (762134, 639069, 614491, 3883100, 4251801, 598114, 606303, 778334),
-    (770264, 712802, 737373, 688221, 639265, 729165, 98, 729175),
-    (802913, 688223, 606289, 770136, 1098250, 737368, 0, 745545),
-    (614490, 745561, 92, 745544, 786709, 761937, 0, 90),
-    (630875, 770133, 0, 77, 811534, 606287, 0, 0),
-    (663639, 704602, 0, 0, 2211915, 94, 0, 0),
-    (89, 0, 0, 0, 704596, 0, 0, 0),
-    (0, 0, 0, 0, 745560, 0, 0, 0),
-    (0, 0, 0, 0, 647260, 0, 0, 0),
-    (0, 0, 0, 0, 737367, 0, 0, 0),
-    (0, 0, 0, 0, 761950, 0, 0, 0),
+    (2113797, 2113793, 2138375, 2130183, 2138375, 2105602, 8438791, 8446981),
+    (4202758, 4194564, 8388866, 8388865, 8438019, 8438016, 16786436, 8406016),
+    (4235780, 4235783, 8438787, 25207814, 8389636, 8422407, 16820227, 3449862),
+    (8446982, 8422406, 16820231, 16803841, 16836613, 16820227, 35202048, 5439626),
+    (16819200, 16835589, 10520577, 8405254, 2099201, 8429830, 7660546, 1123332),
+    (16803841, 16787461, 5506305, 5506307, 2147329, 8388871, 35217551, 5497767),
+    (4194567, 29384966, 9547983, 35233929, 5555202, 1172134, 35234457, 1115137),
+    (10520067, 8397316, 5529862, 2139145, 11661517, 10612939, 7652367, 5481376),
+    (1364173, 35250598, 9523405, 35201702, 1155748, 1147559, 3678349, 3425283),
+    (2105862, 4244482, 5554432, 8396938, 8417487, 2199757, 8430236, 4472974),
+    (9760969, 35234212, 1167561, 5546250, 35201293, 5538819, 1139139, 8470683),
+    (4251907, 1352193, 10601118, 1151179, 5505183, 5791881, 1614756, 1171878),
+    (1315019, 13832393, 5537935, 2097822, 5808266, 8397065, 8397469, 4415644),
+    (2098328, 1336717, 1278663, 1163938, 8429834, 1163920, 1114528, 3441695),
+    (9560600, 1298635, 8618255, 9691845, 1147025, 2212517, 4391064, 4489367),
+    (1613987, 8634918, 5513413, 1425666, 1630881, 1614887, 1328131, 8462494),
+    (2220187, 1630607, 1245324, 1335489, 8528140, 1138847, 1269902, 1212833),
+    (1164827, 1286305, 8585475, 1278495, 5521566, 8487584, 8495650, 1253926),
+    (1343681, 8512037, 1122844, 12812582, 1581193, 5431589, 1237423, 1188884),
+    (2211998, 1613986, 1581229, 1597609, 8462596, 1433741, 8478878, 4465059),
+    (8503846, 13812104, 2408637, 1532076, 1163412, 2188311, 7643285, 8675504),
+    (1630377, 1597633, 4563998, 4481321, 8470703, 4579480, 8560799, 3489942),
+    (1228995, 1130680, 1392779, 1220769, 5472559, 11681955, 1196961, 1557022),
+    (4514080, 4432026, 2179225, 2270344, 1114787, 4481173, 8536752, 3662871),
+    (1401886, 1418250, 4400143, 9626177, 8618254, 1319048, 1212835, 4399533),
+    (1278136, 1548686, 1425544, 9674943, 5546133, 8560900, 4481203, 8618173),
+    (2384414, 8503853, 8487066, 4710702, 2392214, 4366490, 1147932, 1204649),
+    (1147926, 1147070, 4538635, 9568444, 1180694, 1630346, 1556909, 1425968),
+    (1564847, 4382871, 1540247, 2401432, 1237169, 8659205, 8553011, 3572753),
+    (8618543, 1434636, 1228948, 1376792, 8577329, 1409171, 3498423, 4481178),
+    (1532296, 1212553, 8462634, 1228943, 1139354, 1425953, 8454335, 8569013),
+    (3334297, 8462895, 1507866, 1499404, 8560809, 2204691, 1229749, 1147331),
+    (8454658, 3236278, 1269928, 9757224, 1286401, 1499804, 8609974, 1614403),
+    (1212846, 12746907, 4760601, 5742888, 1425578, 4407473, 1409458, 1156120),
+    (3253273, 3293610, 1401022, 2375835, 2171933, 2163740, 8504007, 1434039),
+    (5546174, 4481209, 3276957, 1441933, 5735065, 1286302, 5734841, 1221640),
+    (8495241, 3523610, 4686850, 1557019, 8519826, 1458707, 8585370, 5825212),
+    (13770934, 1499559, 3399855, 2490521, 1376520, 2499613, 5669001, 1180691),
+    (1540235, 8610330, 8642706, 4587704, 1491091, 5677209, 1188029, 1409457),
+    (9609890, 1220780, 4653494, 9601171, 2434073, 2121910, 1384872, 8602161),
+    (9585064, 8536208, 8536236, 2384050, 1499803, 1229854, 1180347, 1515702),
+    (1515935, 1188777, 4341909, 1630776, 2113714, 4399297, 1450170, 1458363),
+    (9593021, 8528032, 8675497, 1197210, 1401891, 2384045, 1130670, 1138872),
+    (1474989, 3375284, 8528017, 1491250, 1245365, 1188889, 1392824, 1401025),
+    (1450397, 8618165, 5669049, 4776218, 8585506, 4726932, 147, 1466536),
+    (9650352, 1401018, 8601762, 1433739, 1548461, 4604083, 0, 1523858),
+    (1130677, 8544403, 1204927, 1417396, 2187431, 1376522, 0, 0),
+    (1458337, 1302715, 8609968, 1450129, 5760026, 1540659, 0, 0),
+    (1409168, 1458344, 5653523, 1515706, 1556656, 1269936, 0, 0),
+    (1499315, 1441945, 1597607, 1343658, 1475611, 1393341, 0, 0),
+    (1523882, 1564849, 1450165, 1482923, 1409209, 5726392, 0, 0),
+    (0, 1466556, 1523877, 179, 1507523, 1556651, 0, 0),
+    (0, 0, 1532087, 0, 1523891, 1474746, 0, 0),
+    (0, 0, 179, 0, 187, 1515682, 0, 0),
+    (0, 0, 0, 0, 0, 1384639, 0, 0),
 )
 UNITS = (
-    (720, 659, 528, 528, 656, 592, 325, 465),
-    (1106, 1040, 645, 979, 709, 647, 401, 517),
-    (1356, 1228, 967, 1164, 1156, 1043, 652, 716),
-    (1413, 1285, 1107, 1233, 1235, 1094, 784, 902),
-    (1679, 1425, 1348, 1287, 1293, 1352, 839, 978),
-    (1732, 1606, 1426, 1359, 1618, 1426, 974, 1039),
-    (1998, 1682, 1807, 1431, 1671, 1476, 1123, 1187),
-    (2054, 1992, 1955, 1490, 1800, 1888, 1170, 1223),
-    (2133, 2052, 2145, 1669, 2057, 1925, 1231, 1296),
-    (2195, 2317, 2188, 1796, 2146, 2209, 1428, 1357),
-    (2440, 2375, 2327, 1891, 2193, 2316, 1491, 1555),
-    (2524, 2447, 2382, 1929, 2316, 2459, 1801, 1611),
-    (2631, 2633, 2440, 2080, 2593, 2574, 1877, 1742),
-    (2720, 2780, 2502, 2118, 2630, 2647, 1924, 1941),
-    (2826, 2848, 2581, 2254, 2709, 2763, 2135, 1994),
-    (2889, 2890, 2654, 2399, 2847, 2836, 2184, 2140),
-    (2975, 3043, 2697, 2453, 3097, 2901, 2396, 2274),
-    (3030, 3096, 2783, 2529, 3210, 2972, 2509, 2390),
-    (3092, 3147, 2838, 2762, 3470, 3107, 2585, 2592),
-    (3171, 3233, 2912, 2850, 3744, 3167, 2657, 2849),
-    (3357, 3293, 2964, 2966, 3875, 3222, 2718, 2884),
-    (3416, 3342, 3042, 3161, 3915, 3298, 2781, 3032),
-    (3486, 3426, 3097, 3211, 4052, 3337, 2827, 3092),
-    (3553, 3479, 3149, 3292, 4118, 3405, 2912, 3165),
-    (3618, 3551, 3224, 3354, 4184, 3481, 2971, 3208),
-    (3674, 3604, 3291, 3421, 4251, 3544, 3014, 3294),
-    (3723, 3673, 3339, 3476, 4316, 3610, 3096, 3359),
-    (3803, 3739, 3421, 3544, 4367, 3665, 3162, 3415),
-    (3853, 3797, 3482, 3614, 4439, 3741, 3222, 3481),
-    (3927, 3870, 3537, 3656, 4506, 3791, 3295, 3529),
-    (3985, 3930, 3594, 3739, 4574, 3850, 3338, 3611),
-    (4057, 3990, 3676, 3789, 4637, 3934, 3426, 3674),
+    (1427, 1554, 1607, 1890, 1698, 1107, 1043, 900),
+    (2082, 2211, 1763, 1935, 1926, 1569, 1184, 1491),
+    (2311, 2513, 2018, 2144, 2064, 1799, 1377, 1543),
+    (2464, 2658, 2128, 2257, 2211, 1874, 1570, 1742),
+    (2851, 2784, 2310, 2593, 2255, 2082, 1678, 1810),
+    (2913, 2849, 2592, 2896, 2464, 2502, 1868, 1999),
+    (4044, 3271, 2885, 3012, 2695, 3140, 2119, 2128),
+    (4235, 3590, 3020, 3342, 3025, 3216, 2706, 2316),
+    (4311, 3659, 3268, 3860, 3076, 3525, 2767, 2513),
+    (4486, 3908, 3742, 3911, 3274, 3619, 2896, 2763),
+    (4575, 4229, 3851, 4043, 3410, 3785, 3153, 3103),
+    (4626, 4301, 4237, 4243, 3592, 3991, 3210, 3789),
+    (4740, 4572, 4501, 4382, 3723, 4559, 3462, 3930),
+    (5073, 4759, 4558, 4550, 3973, 4750, 3935, 4065),
+    (5130, 4819, 4823, 4767, 4238, 4940, 4107, 4258),
+    (5204, 5019, 4879, 4876, 4375, 5083, 4187, 4358),
+    (5327, 5078, 5206, 5130, 4884, 5259, 4313, 4503),
+    (5404, 5130, 5322, 5411, 5001, 5472, 4374, 4618),
+    (5470, 5384, 5460, 5453, 5197, 5462, 4515, 4702),
+    (5513, 5456, 5576, 5641, 5339, 5640, 4685, 4835),
+    (5710, 5646, 5724, 5659, 5525, 5834, 4804, 4872),
+    (5848, 5722, 5841, 5829, 5644, 5913, 4890, 4952),
+    (5901, 5909, 5983, 5911, 5918, 6232, 4958, 5142),
+    (5978, 5961, 6025, 6038, 5971, 6285, 5140, 5211),
+    (6021, 6109, 6355, 6088, 6232, 6430, 5256, 5468),
+    (6096, 6159, 6433, 6168, 6303, 6613, 5341, 5509),
+    (6216, 6228, 6490, 6301, 6426, 6749, 5400, 5600),
+    (6294, 6348, 6552, 6300, 6550, 6810, 5463, 5653),
+    (6361, 6488, 6610, 6418, 6625, 6929, 5509, 5716),
+    (6427, 6559, 6747, 6485, 6684, 6940, 5596, 5785),
+    (6485, 6622, 6813, 6554, 6745, 7007, 5653, 5833),
+    (6557, 6681, 6873, 6617, 6877, 7060, 5705, 5917),
 )
-OPEN = (10, 9, 7, 7, 9, 8, 4, 5)
-MOST = 13
+OPEN = (16, 16, 11, 11, 13, 12, 7, 5)
+MOST = 23
 PARTS = 4
 BACK = 8
 THROUGH = 9
@@ -135,9 +154,11 @@
     last_here = PARTS * jnp.where(z > 0, jnp.int32(BACK), jnp.minimum(chip, BACK)) + PARTS - 1
 
     def clear(slot, c):
-        parts[slot] = jnp.zeros((4 * BLK, HD), jnp.bfloat16)
+        parts[slot] = jnp.zeros((2 * BLK, HD), jnp.bfloat16)
         return c
-    lax.fori_loop(last_here + 1, (BACK + 1) * PARTS, clear, 0)
+    lax.fori_loop(2 * (last_here + 1), 2 * (BACK + 1) * PARTS, clear, 0)
+    for p in range(PARTS):
+        clear(2 * (BACK * PARTS + p), 0)
 
     barrier = pltpu.get_barrier_semaphore()
 
@@ -178,15 +199,14 @@
     kf[...] = k_in[...].astype(jnp.float32).reshape(tokens * kv_heads, HD)
     loads[1].wait()
     vf[...] = v_in[...].astype(jnp.float32).reshape(tokens * kv_heads, HD)
-    mine = pl.multiple_of(core * 2 * BLK, 2 * BLK)
     for p in range(PARTS):
         head = pl.ds(other * PARTS + p, tokens, stride=kv_heads)
         give_kv[p, pl.ds(0, BLK), :] = kf[head, :].astype(jnp.bfloat16)
         give_kv[p, pl.ds(BLK, BLK), :] = vf[head, :].T.astype(jnp.bfloat16)
     for p in range(PARTS):
         head = pl.ds(core * PARTS + p, tokens, stride=kv_heads)
-        parts[p, pl.ds(mine, BLK), :] = kf[head, :].astype(jnp.bfloat16)
-        parts[p, pl.ds(mine + BLK, BLK), :] = vf[head, :].T.astype(jnp.bfloat16)
+        parts[2 * p + core, pl.ds(0, BLK), :] = kf[head, :].astype(jnp.bfloat16)
+        parts[2 * p + core, pl.ds(BLK, BLK), :] = vf[head, :].T.astype(jnp.bfloat16)
 
     pl.semaphore_wait(barrier, greeted)
 
@@ -199,7 +219,7 @@
         pltpu.make_async_copy(ref, ref, sem).wait()
 
     for p in range(PARTS):
-        send(give_kv.at[p], parts.at[p, pl.ds(mine, 2 * BLK)], kv_send, kv_sem.at[p], pair)
+        send(give_kv.at[p], parts.at[2 * p + core], kv_send, kv_sem.at[p], pair)
 
     loads[2].wait()
     qf[...] = q_in[...].astype(jnp.float32).reshape(tokens * q_heads, HD)
@@ -241,14 +261,14 @@
     ones = jnp.ones((16, 2 * BLK), jnp.bfloat16)
 
     def score(slot, p, into):
-        keys = jnp.concatenate([parts[slot, pl.ds(0, BLK), :], parts[slot, pl.ds(2 * BLK, BLK), :]], axis=0)
+        keys = jnp.concatenate([parts[2 * slot, pl.ds(0, BLK), :], parts[2 * slot + 1, pl.ds(0, BLK), :]], axis=0)
         keys = jnp.concatenate([keys, keys], axis=1)
         for b in range(2):
             at_rows = pl.ds(b * rows, rows)
             into[:, at_rows] = jnp.dot(keys, qs[p, :, at_rows], preferred_element_type=jnp.float32)
 
     def combine(slot, p, scores, biases, causal=None):
-        values = jnp.concatenate([parts[slot, pl.ds(BLK, BLK), :], parts[slot, pl.ds(3 * BLK, BLK), :]], axis=1)
+        values = jnp.concatenate([parts[2 * slot, pl.ds(BLK, BLK), :], parts[2 * slot + 1, pl.ds(BLK, BLK), :]], axis=1)
         values = jnp.concatenate([values, ones], axis=0)
         for b in range(2):
             at_rows = pl.ds(b * rows, rows)
@@ -285,23 +305,24 @@
 
     def step(s, sent):
         word = pick(steps, s >> 1) >> (13 * (s & 1))
-        slot = word & 63
+        block = word & 127
+        slot = block >> 1
         here = (slot <= last_here) | ((slot >= THROUGH * PARTS) & has_beyond)
-        ways = jnp.where(here, (word >> 7) & open_ways, 0)
-
-        @pl.when(here & ((word & 64) != 0))
+        ways = jnp.where(here, (word >> 8) & open_ways, 0)
+
+        @pl.when(here & ((word & 128) != 0))
         def _():
-            await_copy(parts.at[slot], part_sem.at[slot])
+            await_copy(parts.at[block], part_sem.at[block])
 
         @pl.when(ways != 0)
         def _():
             for d in range(DIRS):
                 @pl.when((ways & (1 << d)) != 0)
                 def _():
-                    to = slot + shifts[d]
-                    send(parts.at[slot], parts.at[to], send_sem.at[d], part_sem.at[to], targets[d])
+                    to = block + 2 * shifts[d]
+                    send(parts.at[block], parts.at[to], send_sem.at[d], part_sem.at[to], targets[d])
         for d in range(DIRS):
-            sent = sent + (((ways >> d) & 1) << (5 * d))
+            sent = sent + (((ways >> d) & 1) << (6 * d))
         return sent
 
     def unit(u, now, sent, before, scores, scores_before):
@@ -346,15 +367,16 @@
 
     for p in range(PARTS):
         for r in range(group):
-            give_out[p, pl.ds(r * tokens, tokens), :] = result(p, r, other)
-        send(give_out.at[p], o_ref.at[core * PARTS + p], out_send, out_sem, pair)
+            give_out[p, :, pl.ds(r * HD, HD)] = result(p, r, other)
+        send(give_out.at[p], o_ref.at[:, pl.ds(pl.multiple_of((core * PARTS + p) * rows, rows), rows)], out_send, out_sem, pair)
     for p in range(PARTS):
         for r in range(group):
-            o_ref[core * PARTS + p, pl.ds(r * tokens, tokens), :] = result(p, r, core)
+            place = pl.ds(pl.multiple_of((core * PARTS + p) * rows + r * HD, HD), HD)
+            o_ref[:, place] = result(p, r, core)
 
     for d in range(DIRS):
         for n in range(1, MOST + 1):
-            @pl.when(((sent >> (5 * d)) & 31) == n)
+            @pl.when(((sent >> (6 * d)) & 63) == n)
             def _():
                 await_copy(parts.at[pl.ds(0, n)], send_sem.at[d])
     await_copy(give_kv, kv_send)
@@ -371,9 +393,9 @@
     bf16, f32 = jnp.bfloat16, jnp.float32
     anywhere = pl.BlockSpec(memory_space=pl.ANY)
     dma = pltpu.SemaphoreType.DMA
-    by_head = pl.pallas_call(
+    flat = pl.pallas_call(
         kernel,
-        out_shape=jax.ShapeDtypeStruct((kv_heads, rows, HD), bf16),
+        out_shape=jax.ShapeDtypeStruct((tokens, q_heads * HD), bf16),
         in_specs=[anywhere] * 4,
         out_specs=pl.BlockSpec(memory_space=pltpu.VMEM),
         scratch_shapes=[
@@ -381,10 +403,10 @@
             pltpu.VMEM(keys.shape, bf16),
             pltpu.VMEM(values.shape, bf16),
             pltpu.SMEM(doc_blocks.shape, jnp.int32),
-            pltpu.VMEM(((THROUGH + 1) * PARTS, 4 * BLK, HD), bf16),
+            pltpu.VMEM(((THROUGH + 1) * PARTS * 2, 2 * BLK, HD), bf16),
             pltpu.VMEM((PARTS, 2 * BLK, HD), bf16),
             pltpu.VMEM((PARTS, HD, rows), bf16),
-            pltpu.VMEM((PARTS, rows, HD), bf16),
+            pltpu.VMEM((PARTS, tokens, group * HD), bf16),
             pltpu.VMEM((PARTS, HD, rows), bf16),
             pltpu.VMEM((tokens * q_heads, HD), f32),
             pltpu.VMEM((tokens * kv_heads, HD), f32),
@@ -396,7 +418,7 @@
             pltpu.VMEM((2 * BLK, 2 * rows), f32),
             dma((4,)),
             dma((DIRS,)),
-            dma(((THROUGH + 1) * PARTS,)),
+            dma(((THROUGH + 1) * PARTS * 2,)),
             dma,
             dma((PARTS,)),
             dma,
@@ -409,8 +431,7 @@
         ),
         name="attend",
     )(queries, keys, values, doc_blocks)
-    by_head = by_head.reshape(q_heads, tokens, HD)
-    return jnp.transpose(by_head, (1, 0, 2))
+    return flat.reshape(queries.shape)
 
 
 def solution(mesh):

time: 53.9 us -> 49.3 us (0.915)
  Pallas kernels: 50.9 us -> 46.8 us
    pallas_call x1, Pallas kernels: 50.9 us -> 46.8 us  [on_device(): pl.pallas_call(kernel, out_shape=jax.ShapeDtypeStruct((tokens, q_heads *...]
    reshape x1 -> x0, local copies, waits for them, and re-layouts: 2.87 us -> none  [on_device(): by_head = by_head.reshape(q_heads, tokens, HD)]
    unnamed x0 -> x1, local copies, waits for them, and re-layouts: none -> 2.43 us
where the time goes in v4:
time: 49.3 us; the launch traced here: 49.2 us
  Pallas kernels  46.8 us (95%)
  local copies, waits for them, and re-layouts  2.43 us (5%)
    pallas_call x1, Pallas kernels, on_device(): pl.pallas_call(kernel, out_shape=jax.ShapeDtypeStruct((tokens, q_heads *...  46.8 us
    unnamed x1, local copies, waits for them, and re-layouts  2.43 us

profile of v4, /device:TPU:99, one launch (start us, length us, event | category | flops | bytes accessed | tf_op | source)
XLA Modules:
  0.0 49.2 jit_solution(2116161824450882069)
XLA Ops:
  0.0 46.8 %attend.1 = bf16[128,4096]{1,0:T(8,128)(2,1)} custom-call(bf16[128,32,128]{2,1,0:T(8,128)(2,1)} %q_hbm.1, bf16[128,8,128]{2,1,0:T(8,128)(2,1)} %k_hbm.1, bf16[128,8,128]{2,1,0:T(8,128)(2,1)} %v_hbm.1, s32[32]{0:T(128)} %docs_hbm.1), custom_call_target="tpu_custom_call" | custom-call | tf_op jit(solution)/shard_map/attend/pallas_call | solution.py:396
  46.8 2.4 %copy.5 = bf16[16,8,32,128]{3,2,1,0:T(8,128)(2,1)} copy(bf16[16,8,32,128]{3,1,2,0:T(8,128)(2,1)} %bitcast.2) | data formatting | bytes 2097152

commit v5 on v4

--- a/solution.py
+++ b/solution.py
@@ -221,29 +221,6 @@
     for p in range(PARTS):
         send(give_kv.at[p], parts.at[2 * p + core], kv_send, kv_sem.at[p], pair)
 
-    loads[2].wait()
-    qf[...] = q_in[...].astype(jnp.float32).reshape(tokens * q_heads, HD)
-
-    def queries_of(p, r, side):
-        return qf[pl.ds((side * PARTS + p) * group + r, tokens, stride=q_heads), :].T
-
-    for p in range(PARTS):
-        for r in range(group):
-            give_q[p, :, pl.ds(r * tokens, tokens)] = queries_of(p, r, other).astype(jnp.bfloat16)
-        send(give_q.at[p], qx.at[p], q_send, q_sem.at[p], pair)
-
-    scale = LOG2E * HD**-0.5
-
-    def put_queries(p, at_rows, value):
-        scaled = value * scale
-        high = scaled.astype(jnp.bfloat16)
-        qs[p, pl.ds(0, HD), at_rows] = high
-        qs[p, pl.ds(HD, HD), at_rows] = (scaled - high.astype(jnp.float32)).astype(jnp.bfloat16)
-
-    for p in range(PARTS):
-        for r in range(group):
-            put_queries(p, pl.ds(pl.multiple_of(core * rows + r * tokens, tokens), tokens), queries_of(p, r, core))
-
     loads[3].wait()
     reach = []
     for b in range(2):
@@ -336,6 +313,32 @@
     for p in range(PARTS):
         await_copy(give_kv.at[p], kv_sem.at[p])
 
+    opening = of_place(OPEN)
+    sent = lax.fori_loop(0, opening, step, jnp.int32(0))
+
+    loads[2].wait()
+    qf[...] = q_in[...].astype(jnp.float32).reshape(tokens * q_heads, HD)
+
+    def queries_of(p, r, side):
+        return qf[pl.ds((side * PARTS + p) * group + r, tokens, stride=q_heads), :].T
+
+    for p in range(PARTS):
+        for r in range(group):
+            give_q[p, :, pl.ds(r * tokens, tokens)] = queries_of(p, r, other).astype(jnp.bfloat16)
+        send(give_q.at[p], qx.at[p], q_send, q_sem.at[p], pair)
+
+    scale = LOG2E * HD**-0.5
+
+    def put_queries(p, at_rows, value):
+        scaled = value * scale
+        high = scaled.astype(jnp.bfloat16)
+        qs[p, pl.ds(0, HD), at_rows] = high
+        qs[p, pl.ds(HD, HD), at_rows] = (scaled - high.astype(jnp.float32)).astype(jnp.bfloat16)
+
+    for p in range(PARTS):
+        for r in range(group):
+            put_queries(p, pl.ds(pl.multiple_of(core * rows + r * tokens, tokens), tokens), queries_of(p, r, core))
+
     def attend_own():
         key = lax.broadcasted_iota(jnp.int32, (BLK, rows), 0)
         query = lax.broadcasted_iota(jnp.int32, (BLK, rows), 1) % tokens
@@ -350,8 +353,6 @@
                 score(p + 1, p + 1, (even, odd)[(p + 1) % 2])
             combine(p, p, (even, odd)[p % 2], biases, causal)
 
-    opening = of_place(OPEN)
-    sent = lax.fori_loop(0, opening, step, jnp.int32(0))
     attend_own()
 
     def two_units(i, state):

time: 49.3 us -> 47.8 us (0.970)
  Pallas kernels: 46.8 us -> 45.3 us
    pallas_call x1, Pallas kernels: 46.8 us -> 45.3 us  [on_device(): pl.pallas_call(kernel, out_shape=jax.ShapeDtypeStruct((tokens, q_heads *...]
where the time goes in v5:
time: 47.8 us; the launch traced here: 47.7 us
  Pallas kernels  45.3 us (95%)
  local copies, waits for them, and re-layouts  2.43 us (5%)
    pallas_call x1, Pallas kernels, on_device(): pl.pallas_call(kernel, out_shape=jax.ShapeDtypeStruct((tokens, q_heads *...  45.3 us
    unnamed x1, local copies, waits for them, and re-layouts  2.43 us

profile of v5, /device:TPU:99, one launch (start us, length us, event | category | flops | bytes accessed | tf_op | source)
XLA Modules:
  0.0 47.7 jit_solution(6807186064767137856)
XLA Ops:
  0.0 45.3 %attend.1 = bf16[128,4096]{1,0:T(8,128)(2,1)} custom-call(bf16[128,32,128]{2,1,0:T(8,128)(2,1)} %q_hbm.1, bf16[128,8,128]{2,1,0:T(8,128)(2,1)} %k_hbm.1, bf16[128,8,128]{2,1,0:T(8,128)(2,1)} %v_hbm.1, s32[32]{0:T(128)} %docs_hbm.1), custom_call_target="tpu_custom_call" | custom-call | tf_op jit(solution)/shard_map/attend/pallas_call | solution.py:397
  45.3 2.4 %copy.5 = bf16[16,8,32,128]{3,2,1,0:T(8,128)(2,1)} copy(bf16[16,8,32,128]{3,1,2,0:T(8,128)(2,1)} %bitcast.2) | data formatting | bytes 2097152

commit v6 on v5

--- a/solution.py
+++ b/solution.py
@@ -6,97 +6,96 @@
 from jax.sharding import PartitionSpec as P
 
 STEPS = (
-    (2113797, 2113793, 2138375, 2130183, 2138375, 2105602, 8438791, 8446981),
-    (4202758, 4194564, 8388866, 8388865, 8438019, 8438016, 16786436, 8406016),
-    (4235780, 4235783, 8438787, 25207814, 8389636, 8422407, 16820227, 3449862),
-    (8446982, 8422406, 16820231, 16803841, 16836613, 16820227, 35202048, 5439626),
-    (16819200, 16835589, 10520577, 8405254, 2099201, 8429830, 7660546, 1123332),
-    (16803841, 16787461, 5506305, 5506307, 2147329, 8388871, 35217551, 5497767),
-    (4194567, 29384966, 9547983, 35233929, 5555202, 1172134, 35234457, 1115137),
-    (10520067, 8397316, 5529862, 2139145, 11661517, 10612939, 7652367, 5481376),
-    (1364173, 35250598, 9523405, 35201702, 1155748, 1147559, 3678349, 3425283),
-    (2105862, 4244482, 5554432, 8396938, 8417487, 2199757, 8430236, 4472974),
-    (9760969, 35234212, 1167561, 5546250, 35201293, 5538819, 1139139, 8470683),
-    (4251907, 1352193, 10601118, 1151179, 5505183, 5791881, 1614756, 1171878),
-    (1315019, 13832393, 5537935, 2097822, 5808266, 8397065, 8397469, 4415644),
-    (2098328, 1336717, 1278663, 1163938, 8429834, 1163920, 1114528, 3441695),
-    (9560600, 1298635, 8618255, 9691845, 1147025, 2212517, 4391064, 4489367),
-    (1613987, 8634918, 5513413, 1425666, 1630881, 1614887, 1328131, 8462494),
-    (2220187, 1630607, 1245324, 1335489, 8528140, 1138847, 1269902, 1212833),
-    (1164827, 1286305, 8585475, 1278495, 5521566, 8487584, 8495650, 1253926),
-    (1343681, 8512037, 1122844, 12812582, 1581193, 5431589, 1237423, 1188884),
-    (2211998, 1613986, 1581229, 1597609, 8462596, 1433741, 8478878, 4465059),
-    (8503846, 13812104, 2408637, 1532076, 1163412, 2188311, 7643285, 8675504),
-    (1630377, 1597633, 4563998, 4481321, 8470703, 4579480, 8560799, 3489942),
-    (1228995, 1130680, 1392779, 1220769, 5472559, 11681955, 1196961, 1557022),
-    (4514080, 4432026, 2179225, 2270344, 1114787, 4481173, 8536752, 3662871),
-    (1401886, 1418250, 4400143, 9626177, 8618254, 1319048, 1212835, 4399533),
-    (1278136, 1548686, 1425544, 9674943, 5546133, 8560900, 4481203, 8618173),
-    (2384414, 8503853, 8487066, 4710702, 2392214, 4366490, 1147932, 1204649),
-    (1147926, 1147070, 4538635, 9568444, 1180694, 1630346, 1556909, 1425968),
-    (1564847, 4382871, 1540247, 2401432, 1237169, 8659205, 8553011, 3572753),
-    (8618543, 1434636, 1228948, 1376792, 8577329, 1409171, 3498423, 4481178),
-    (1532296, 1212553, 8462634, 1228943, 1139354, 1425953, 8454335, 8569013),
-    (3334297, 8462895, 1507866, 1499404, 8560809, 2204691, 1229749, 1147331),
-    (8454658, 3236278, 1269928, 9757224, 1286401, 1499804, 8609974, 1614403),
-    (1212846, 12746907, 4760601, 5742888, 1425578, 4407473, 1409458, 1156120),
-    (3253273, 3293610, 1401022, 2375835, 2171933, 2163740, 8504007, 1434039),
-    (5546174, 4481209, 3276957, 1441933, 5735065, 1286302, 5734841, 1221640),
-    (8495241, 3523610, 4686850, 1557019, 8519826, 1458707, 8585370, 5825212),
-    (13770934, 1499559, 3399855, 2490521, 1376520, 2499613, 5669001, 1180691),
-    (1540235, 8610330, 8642706, 4587704, 1491091, 5677209, 1188029, 1409457),
-    (9609890, 1220780, 4653494, 9601171, 2434073, 2121910, 1384872, 8602161),
-    (9585064, 8536208, 8536236, 2384050, 1499803, 1229854, 1180347, 1515702),
-    (1515935, 1188777, 4341909, 1630776, 2113714, 4399297, 1450170, 1458363),
-    (9593021, 8528032, 8675497, 1197210, 1401891, 2384045, 1130670, 1138872),
-    (1474989, 3375284, 8528017, 1491250, 1245365, 1188889, 1392824, 1401025),
-    (1450397, 8618165, 5669049, 4776218, 8585506, 4726932, 147, 1466536),
-    (9650352, 1401018, 8601762, 1433739, 1548461, 4604083, 0, 1523858),
-    (1130677, 8544403, 1204927, 1417396, 2187431, 1376522, 0, 0),
-    (1458337, 1302715, 8609968, 1450129, 5760026, 1540659, 0, 0),
-    (1409168, 1458344, 5653523, 1515706, 1556656, 1269936, 0, 0),
-    (1499315, 1441945, 1597607, 1343658, 1475611, 1393341, 0, 0),
-    (1523882, 1564849, 1450165, 1482923, 1409209, 5726392, 0, 0),
-    (0, 1466556, 1523877, 179, 1507523, 1556651, 0, 0),
-    (0, 0, 1532087, 0, 1523891, 1474746, 0, 0),
-    (0, 0, 179, 0, 187, 1515682, 0, 0),
-    (0, 0, 0, 0, 0, 1384639, 0, 0),
+    (2130179, 2105602, 2138372, 2138370, 2097410, 2105606, 8406019, 8422402),
+    (4194565, 4210950, 8413441, 8438019, 8413441, 8446210, 16786438, 16802816),
+    (4235783, 12608000, 8438786, 8389636, 8446982, 8414210, 16820231, 8446982),
+    (8406022, 25224198, 16820225, 16836611, 10520577, 2123781, 8430596, 1164194),
+    (16802823, 16787461, 8446211, 2148357, 8429830, 2155520, 35201443, 5460171),
+    (16787461, 4202757, 2114560, 10544129, 1147555, 5563396, 5439626, 3441678),
+    (4203266, 8430596, 5529739, 5554314, 10588361, 3231949, 8474831, 5439625),
+    (35217670, 2155014, 8483017, 8409291, 1155750, 1156101, 35233928, 1131529),
+    (2106022, 1339599, 5521664, 1122561, 5563661, 2204322, 5497250, 3695520),
+    (3428557, 2384391, 1151181, 35250852, 1581193, 1262593, 1123335, 8430235),
+    (9757188, 1360898, 8487174, 35234052, 2171024, 1139363, 3679142, 7651467),
+    (9662665, 8679629, 5554317, 5506058, 8708624, 1196229, 8389277, 8413849),
+    (4219143, 4505860, 5464769, 5496974, 11625124, 8601867, 5538247, 3465359),
+    (1598603, 35201191, 8495367, 2097859, 5546135, 5505166, 1613964, 4513950),
+    (1131674, 1344670, 1368202, 1156105, 1294474, 2212875, 4759706, 3523585),
+    (4407563, 2417156, 1613982, 1630881, 4440357, 5538448, 3449864, 1302674),
+    (8470725, 1630346, 4440330, 2203802, 1115173, 2416783, 1253518, 8536622),
+    (2179271, 9666725, 1164315, 1173018, 2122412, 5440530, 8462885, 3481749),
+    (9683462, 2392226, 1302688, 1613991, 1221655, 1122469, 1212842, 4440254),
+    (1163457, 1147397, 4448551, 2359451, 1163437, 2171429, 1557034, 1205269),
+    (3629598, 1615000, 1401895, 1328667, 8560906, 1205264, 3466241, 1278373),
+    (8503481, 2195592, 1114249, 1245355, 1172124, 4350113, 1278101, 1230373),
+    (1401001, 8454691, 2449952, 4391211, 1548999, 10608780, 8561214, 1286563),
+    (13787433, 9625795, 1393672, 1393678, 8618248, 1114270, 3408017, 8544803),
+    (1523887, 3498177, 9667244, 1114252, 1400978, 2130106, 1270311, 1434017),
+    (1156246, 1557028, 1171723, 4776225, 8536327, 8503866, 3474449, 4448443),
+    (5431722, 9552059, 1286829, 1385505, 5808797, 1220753, 4456595, 3556391),
+    (3294231, 1540389, 8634658, 4513967, 2212015, 2138795, 8487090, 1540241),
+    (9633982, 1253916, 1532051, 9666863, 1328136, 1303582, 1384877, 8471090),
+    (3522959, 1172505, 4513942, 1523884, 3564215, 1376434, 4522281, 3580055),
+    (9503396, 2179256, 2253829, 2458140, 1483446, 2507807, 8601758, 4702388),
+    (5546163, 9585176, 5824658, 1213584, 2220179, 5636774, 1138849, 3712025),
+    (1492112, 1376406, 2580644, 4530363, 5735583, 2490547, 2367670, 1441932),
+    (1220767, 5398798, 1377289, 1287444, 2482346, 1229836, 8544809, 8659525),
+    (1564855, 1188883, 1212611, 1466542, 9660056, 1384623, 1196213, 3563691),
+    (1508497, 2236599, 2245156, 12820795, 2138290, 5480751, 4423989, 4423821),
+    (3220636, 8519824, 1450172, 1417355, 1598112, 1499310, 8585387, 3728415),
+    (9535912, 1425549, 4358335, 2515137, 5513384, 5464356, 7741584, 4628666),
+    (3540125, 1564983, 1556774, 1540786, 1261759, 1474750, 8593583, 1393686),
+    (1253556, 1139729, 9609394, 2465938, 1212600, 1237285, 3506319, 8626616),
+    (1483185, 2220217, 4686130, 1228963, 7823534, 9667263, 8643260, 5710007),
+    (1540244, 3219615, 9650341, 9683376, 1524393, 1392908, 1228986, 1410065),
+    (1335469, 9601202, 2212541, 5670041, 1228980, 1597612, 4399293, 1418177),
+    (1458348, 1467546, 1385623, 5742760, 1441937, 1491200, 1467406, 1212607),
+    (1310909, 2474145, 2425007, 1237439, 1556633, 1540283, 4465083, 1114294),
+    (161, 3540381, 5677238, 11673749, 1515697, 5742880, 1238036, 1376445),
+    (0, 1417365, 2539694, 1491646, 0, 2162869, 8520120, 1450128),
+    (0, 1392817, 1475258, 3612819, 0, 1507476, 7807159, 0),
+    (0, 1474715, 1499441, 1499301, 0, 1630381, 1155263, 0),
+    (0, 1433772, 1187984, 1507505, 0, 1253553, 1597614, 0),
+    (0, 1482938, 1253528, 181, 0, 1581241, 1441972, 0),
+    (0, 1548448, 1507504, 0, 0, 0, 0, 0),
+    (0, 1384630, 1515699, 0, 0, 0, 0, 0),
+    (0, 0, 161, 0, 0, 0, 0, 0),
 )
 UNITS = (
-    (1427, 1554, 1607, 1890, 1698, 1107, 1043, 900),
-    (2082, 2211, 1763, 1935, 1926, 1569, 1184, 1491),
-    (2311, 2513, 2018, 2144, 2064, 1799, 1377, 1543),
-    (2464, 2658, 2128, 2257, 2211, 1874, 1570, 1742),
-    (2851, 2784, 2310, 2593, 2255, 2082, 1678, 1810),
-    (2913, 2849, 2592, 2896, 2464, 2502, 1868, 1999),
-    (4044, 3271, 2885, 3012, 2695, 3140, 2119, 2128),
-    (4235, 3590, 3020, 3342, 3025, 3216, 2706, 2316),
-    (4311, 3659, 3268, 3860, 3076, 3525, 2767, 2513),
-    (4486, 3908, 3742, 3911, 3274, 3619, 2896, 2763),
-    (4575, 4229, 3851, 4043, 3410, 3785, 3153, 3103),
-    (4626, 4301, 4237, 4243, 3592, 3991, 3210, 3789),
-    (4740, 4572, 4501, 4382, 3723, 4559, 3462, 3930),
-    (5073, 4759, 4558, 4550, 3973, 4750, 3935, 4065),
-    (5130, 4819, 4823, 4767, 4238, 4940, 4107, 4258),
-    (5204, 5019, 4879, 4876, 4375, 5083, 4187, 4358),
-    (5327, 5078, 5206, 5130, 4884, 5259, 4313, 4503),
-    (5404, 5130, 5322, 5411, 5001, 5472, 4374, 4618),
-    (5470, 5384, 5460, 5453, 5197, 5462, 4515, 4702),
-    (5513, 5456, 5576, 5641, 5339, 5640, 4685, 4835),
-    (5710, 5646, 5724, 5659, 5525, 5834, 4804, 4872),
-    (5848, 5722, 5841, 5829, 5644, 5913, 4890, 4952),
-    (5901, 5909, 5983, 5911, 5918, 6232, 4958, 5142),
-    (5978, 5961, 6025, 6038, 5971, 6285, 5140, 5211),
-    (6021, 6109, 6355, 6088, 6232, 6430, 5256, 5468),
-    (6096, 6159, 6433, 6168, 6303, 6613, 5341, 5509),
-    (6216, 6228, 6490, 6301, 6426, 6749, 5400, 5600),
-    (6294, 6348, 6552, 6300, 6550, 6810, 5463, 5653),
-    (6361, 6488, 6610, 6418, 6625, 6929, 5509, 5716),
-    (6427, 6559, 6747, 6485, 6684, 6940, 5596, 5785),
-    (6485, 6622, 6813, 6554, 6745, 7007, 5653, 5833),
-    (6557, 6681, 6873, 6617, 6877, 7060, 5705, 5917),
+    (1427, 1747, 1169, 1761, 1030, 1361, 1105, 1185),
+    (1825, 2211, 1478, 2000, 1171, 1477, 1284, 1293),
+    (1869, 2322, 1696, 2147, 1312, 1698, 1440, 1413),
+    (2053, 2577, 1861, 2311, 1810, 2119, 1635, 1548),
+    (2210, 2722, 2003, 2515, 1861, 2386, 1826, 1671),
+    (2403, 3041, 2274, 2658, 2180, 2697, 2066, 1875),
+    (2528, 3168, 2447, 2765, 2518, 2896, 2188, 2063),
+    (3229, 3724, 2820, 3093, 2823, 2950, 2707, 2569),
+    (3413, 3847, 3093, 3142, 2915, 3140, 2762, 2642),
+    (3467, 4171, 3335, 3396, 3406, 3400, 2958, 2897),
+    (3593, 4361, 3478, 4189, 3554, 3727, 3213, 2958),
+    (3783, 4680, 3598, 4366, 3729, 4051, 3732, 3152),
+    (3863, 4806, 4041, 4503, 3931, 4185, 3919, 3223),
+    (4114, 5023, 4195, 4677, 4041, 4500, 4048, 3787),
+    (4303, 5125, 4449, 4822, 4175, 4695, 4101, 3930),
+    (4443, 5276, 5023, 4896, 4318, 4877, 4489, 4130),
+    (4511, 5327, 5130, 5081, 4373, 5131, 4693, 4505),
+    (4552, 5444, 5330, 5201, 4569, 5279, 4808, 4550),
+    (4636, 5657, 5453, 5391, 4769, 5326, 5063, 4771),
+    (4740, 5838, 5534, 5516, 4880, 5525, 5142, 4829),
+    (4820, 5962, 5707, 5588, 5005, 5601, 5470, 5013),
+    (4870, 6104, 5780, 5726, 5130, 5723, 5657, 5276),
+    (5006, 6165, 5975, 5771, 5271, 5853, 5725, 5472),
+    (5132, 6221, 6109, 5898, 5332, 5982, 5899, 5526),
+    (5208, 6358, 6170, 6024, 5405, 6042, 6107, 5599),
+    (5274, 6423, 6299, 6175, 5466, 6154, 6172, 5642),
+    (5386, 6493, 6408, 6217, 5515, 6230, 6239, 5723),
+    (5585, 6554, 6540, 6290, 5576, 6307, 6278, 5764),
+    (5718, 6672, 6616, 6427, 5708, 6360, 6359, 5918),
+    (5785, 6750, 6745, 6424, 5791, 6412, 6433, 5972),
+    (5854, 6747, 6812, 6428, 5848, 6492, 6490, 6024),
+    (5840, 6804, 6864, 6490, 5916, 6560, 6552, 6040),
 )
-OPEN = (16, 16, 11, 11, 13, 12, 7, 5)
+OPEN = (15, 16, 12, 12, 10, 11, 8, 6)
 MOST = 23
 PARTS = 4
 BACK = 8

time: 47.8 us -> 47.9 us (level)
  no operation moved by 1% of the time
where the time goes in v6:
time: 47.9 us; the launch traced here: 47.8 us
  Pallas kernels  45.3 us (95%)
  local copies, waits for them, and re-layouts  2.43 us (5%)
    pallas_call x1, Pallas kernels, on_device(): pl.pallas_call(kernel, out_shape=jax.ShapeDtypeStruct((tokens, q_heads *...  45.3 us
    unnamed x1, local copies, waits for them, and re-layouts  2.43 us

profile of v6, /device:TPU:99, one launch (start us, length us, event | category | flops | bytes accessed | tf_op | source)
XLA Modules:
  0.0 47.8 jit_solution(6075370265743582677)
XLA Ops:
  0.0 45.3 %attend.1 = bf16[128,4096]{1,0:T(8,128)(2,1)} custom-call(bf16[128,32,128]{2,1,0:T(8,128)(2,1)} %q_hbm.1, bf16[128,8,128]{2,1,0:T(8,128)(2,1)} %k_hbm.1, bf16[128,8,128]{2,1,0:T(8,128)(2,1)} %v_hbm.1, s32[32]{0:T(128)} %docs_hbm.1), custom_call_target="tpu_custom_call" | custom-call | tf_op jit(solution)/shard_map/attend/pallas_call | solution.py:396
  45.3 2.4 %copy.5 = bf16[16,8,32,128]{3,2,1,0:T(8,128)(2,1)} copy(bf16[16,8,32,128]{3,1,2,0:T(8,128)(2,1)} %bitcast.2) | data formatting | bytes 2097152
